TPU v7x, 128 devices: a whole 4x4x4 slice. The times are simulated.
128 devices in a mesh: dp: 16 (over y, z_hi, core), tensor: 8 (over z_lo, x).
Axes of the slice: x: 4, y: 4, z: 4 (z_hi: 2, z_lo: 2; z = z_hi * 2 + z_lo), core: 2. Of those that a mesh axis runs over, the one named last changes fastest.
Arguments:
- tag_ids: int32 [128, 8], P(('dp', 'tensor')), may hold values from 0 to 127
- tag_amounts: float32 [128, 8], P(('dp', 'tensor')), may hold values from 0.05 to 1
- tag_table: bfloat16 [128, 256], replicated, may hold values from -6 to 6
- position_table: bfloat16 [32, 256], replicated, may hold values from -6 to 6
- prefix_weight: bfloat16 [256, 2048], replicated, may hold values from -0.75 to 0.75
- query_own: bfloat16 [128, 768, 4096], P('dp', None, 'tensor'), may hold values from -9 to 9
- key_own: bfloat16 [128, 768, 1024], P('dp', None, 'tensor'), may hold values from -6 to 6
- value_own: bfloat16 [128, 768, 1024], P('dp', None, 'tensor'), may hold values from -6 to 6
- out_grad: bfloat16 [128, 768, 4096], P('dp', None, 'tensor'), may hold values from -6 to 6
- seq_lengths: int32 [128], P('dp'), may hold values from 384 to 768, as said below
Outputs:
- attn_out: bfloat16 [128, 768, 4096], P('dp', None, 'tensor')
- prefix_grad: float32 [128, 32, 2048], P(('dp', 'tensor'))
- weight_grad: float32 [256, 2048], replicated
Inputs may be any that keep to these rules, and one draw needn't show every extreme that they name: `seq_lengths`: some sequence is full in every draw.
All inputs are finite; a program needn't handle non-finite values.
Results may differ from a plain program's by a relative error of at most 0.0082.
Values may be sent and summed in bfloat16 or wider, within the bound.
A program may use at most 128 MiB of HBM per device.

v0:
```python
import jax
import jax.numpy as jnp
from jax import lax
from jax.sharding import PartitionSpec as P

HD = 128


def encode(tag_ids, tag_amounts, tag_table, position_table):
    onehot = (
        tag_ids[:, :, None] == jnp.arange(tag_table.shape[0], dtype=jnp.int32)[None, None, :]
    ).astype(jnp.float32)
    mixture = (
        jnp.sum(onehot * tag_amounts[:, :, None], axis=1) / jnp.sum(tag_amounts, axis=1)[:, None]
    )
    pooled = jnp.dot(mixture, tag_table.astype(jnp.float32), precision=lax.Precision.HIGHEST)
    return jnp.tanh(position_table.astype(jnp.float32)[None, :, :] + pooled[:, None, :]).astype(
        jnp.bfloat16
    )


def project(hidden, weight_block):
    result = jnp.dot(
        hidden.reshape(-1, hidden.shape[2]), weight_block, preferred_element_type=jnp.float32
    )
    return result.astype(jnp.bfloat16).reshape(hidden.shape[0], hidden.shape[1], -1)


def attend(query, key_own, value_own, prefix, cotangent, length):
    row_count = query.shape[0]
    prefix_len = prefix.shape[0]
    shared_heads = key_own.shape[1] // HD
    group_size = query.shape[1] // (shared_heads * HD)
    score_scale = 1.0 / HD**0.5
    prefix_split = prefix.reshape(prefix_len, shared_heads, 2, HD)
    all_keys = jnp.concatenate(
        [prefix_split[:, :, 0], key_own.reshape(row_count, shared_heads, HD)], 0
    )
    all_values = jnp.concatenate(
        [prefix_split[:, :, 1], value_own.reshape(row_count, shared_heads, HD)], 0
    )
    query_heads = query.reshape(row_count, shared_heads, group_size, HD)
    scores = (
        jnp.einsum("ikgd,jkd->kgij", query_heads, all_keys, preferred_element_type=jnp.float32)
        * score_scale
    )
    row_index = jnp.arange(row_count, dtype=jnp.int32)[:, None]
    col_index = jnp.arange(prefix_len + row_count, dtype=jnp.int32)[None, :] - prefix_len
    allowed = (col_index < 0) | (col_index <= row_index) & (col_index < length)
    scores = jnp.where(allowed, scores, -1e30)
    row_max = jnp.max(scores, axis=-1, keepdims=True)
    exp_scores = jnp.exp(scores - row_max)
    probs = exp_scores / jnp.sum(exp_scores, axis=-1, keepdims=True)
    weights = probs.astype(jnp.bfloat16)
    output = jnp.einsum(
        "kgij,jkd->ikgd", weights, all_values, preferred_element_type=jnp.float32
    ).astype(jnp.bfloat16)
    live_rows = (jnp.arange(row_count, dtype=jnp.int32) < length)[:, None, None, None]
    grad_live = jnp.where(
        live_rows,
        cotangent.reshape(row_count, shared_heads, group_size, HD),
        jnp.zeros((), jnp.bfloat16),
    )
    row_delta = jnp.sum(grad_live.astype(jnp.float32) * output.astype(jnp.float32), axis=-1)
    row_delta = jnp.transpose(row_delta, (1, 2, 0))
    prob_grad = jnp.einsum(
        "ikgd,jkd->kgij", grad_live, prefix_split[:, :, 1], preferred_element_type=jnp.float32
    )
    score_grad = (probs[..., :prefix_len] * (prob_grad - row_delta[..., None])).astype(jnp.bfloat16)
    key_grad = (
        jnp.einsum("kgij,ikgd->jkd", score_grad, query_heads, preferred_element_type=jnp.float32)
        * score_scale
    )
    value_grad = jnp.einsum(
        "kgij,ikgd->jkd", weights[..., :prefix_len], grad_live, preferred_element_type=jnp.float32
    )
    prefix_grads = jnp.stack([key_grad, value_grad], 2).reshape(prefix_len, shared_heads * 2 * HD)
    return (output.reshape(row_count, -1), prefix_grads)


def shards(
    tag_ids,
    tag_amounts,
    tag_table,
    position_table,
    prefix_weight,
    query_own,
    key_own,
    value_own,
    out_grad,
    seq_lengths,
):
    tensor_size = lax.axis_size("tensor")
    hidden = encode(tag_ids, tag_amounts, tag_table, position_table)
    prefix = lax.all_to_all(
        project(hidden, prefix_weight), "tensor", split_axis=2, concat_axis=0, tiled=True
    )

    def one_sequence(items):
        return attend(items[0], items[1], items[2], items[3], items[4], items[5])

    attn_out, prefix_grads = lax.map(
        one_sequence, (query_own, key_own, value_own, prefix, out_grad, seq_lengths)
    )
    prefix_grad = lax.all_to_all(prefix_grads, "tensor", split_axis=0, concat_axis=2, tiled=True)
    example_count = prefix_grad.shape[0] * lax.axis_size("dp") * tensor_size
    flat_hidden = hidden.reshape(-1, hidden.shape[2]).astype(jnp.float32)
    partial_grad = lax.dot_general(
        flat_hidden,
        prefix_grad.reshape(flat_hidden.shape[0], -1),
        (((0,), (0,)), ((), ())),
        precision=lax.Precision.HIGHEST,
    )
    weight_grad = lax.psum(partial_grad, ("dp", "tensor")) / example_count
    return (attn_out, prefix_grad, weight_grad)


def solution(mesh):
    return jax.shard_map(
        shards,
        mesh=mesh,
        in_specs=(
            P(("dp", "tensor"), None),
            P(("dp", "tensor"), None),
            P(),
            P(),
            P(),
            P("dp", None, "tensor"),
            P("dp", None, "tensor"),
            P("dp", None, "tensor"),
            P("dp", None, "tensor"),
            P("dp"),
        ),
        out_specs=(P("dp", None, "tensor"), P(("dp", "tensor"), None, None), P()),
        check_vma=False,
    )
```

profile of v0, /device:TPU:1, one launch (start us, length us, event | category | flops | bytes accessed | tf_op | source)
XLA Modules:
  0.0 445.3 jit_solution(16203584963181482189)
XLA Ops:
  13.2 11.5 %reduce.14 = bf16[2048,32]{1,0:T(8,128)(2,1)S(1)} reduce(bf16[2048,1,32]{2,1,0:T(2,128)(2,1)S(1)} %bitcast.196, bf16[]{:T(256)} %broadcast.196), dimensions={1}, to_apply=%bitcast.121.reduce_sub_computation | reduce | bytes 262146
  25.9 6.2 %all-to-all-start = ((bf16[8,2,4096]{2,1,0:T(2,128)(2,1)}), bf16[8,2,4096]{2,1,0:T(2,128)(2,1)S(1)}, u32[]{:S(2)}, u32[]{:S(2)}) async-start(bf16[8,2,4096]{2,1,0:T(2,128)(2,1)} %reshape.288), calls=%async_computation | async-start | bytes 262144 | tf_op jit(solution)/shard_map/all_to_all | solution.py:95
  32.3 5.2 %all-to-all-done = bf16[8,2,4096]{2,1,0:T(2,128)(2,1)S(1)} async-done(((bf16[8,2,4096]{2,1,0:T(2,128)(2,1)}), bf16[8,2,4096]{2,1,0:T(2,128)(2,1)S(1)}, u32[]{:S(2)}, u32[]{:S(2)}) %all-to-all-start) | async-done | bytes 131104 | tf_op jit(solution)/shard_map/all_to_all | solution.py:95
  39.5 230.8 %while.14 = (s32[]{:T(128)}, bf16[8,768,512]{2,1,0:T(8,128)(2,1)}, f32[8,32,256]{2,1,0:T(8,128)}, bf16[8,32,256]{2,1,0:T(8,128)(2,1)}, bf16[8,768,128]{2,1,0:T(8...) while((s32[]{:T(128)}, bf16[8,768,512]{2,1,0:T(8,128)(2,1)}, ...), condition=%wide.region_6.7_spmd, body=%wide.region_2.6_spmd.sunk | while | flops 1369389952 | bytes 69592584 | solution.py:102
  50.7 6.2 %fusion.72 = (bf16[1,4,768,800]{2,3,1,0:T(8,128)(2,1)}, f32[1,4,768,800]{2,3,1,0:T(8,128)}) fusion(f32[4,768]{1,0:T(4,128)S(1)} %fusion.71, f32[4,768]{1,0:T(4,128)S(1)} %get-tuple-element.293, f32[800,768,4]{1,0,2:T(8,128)S(1)} %get-tuple-element.292, pred[768,800]{0,1:T(8,128)(4,1)S(1)} %fusion.68), kind=kLoop, calls=%fused_computation.66.clone.1 | loop fusion | flops 12288000 | bytes 25214976 | tf_op jit(solution)/shard_map/while/body/eval_jaxpr/convert_element_type | solution.py:54
  59.0 3.5 multiply_reduce_fusion.2
  71.2 2.4 constant_dynamic-slice_fusion.5
  79.6 6.2 %fusion.72 = (bf16[1,4,768,800]{2,3,1,0:T(8,128)(2,1)}, f32[1,4,768,800]{2,3,1,0:T(8,128)}) fusion(f32[4,768]{1,0:T(4,128)S(1)} %fusion.71, f32[4,768]{1,0:T(4,128)S(1)} %get-tuple-element.293, f32[800,768,4]{1,0,2:T(8,128)S(1)} %get-tuple-element.292, pred[768,800]{0,1:T(8,128)(4,1)S(1)} %fusion.68), kind=kLoop, calls=%fused_computation.66.clone.1 | loop fusion | flops 12288000 | bytes 25214976 | tf_op jit(solution)/shard_map/while/body/eval_jaxpr/convert_element_type | solution.py:54
  87.8 3.5 multiply_reduce_fusion.2
  108.4 6.2 %fusion.72 = (bf16[1,4,768,800]{2,3,1,0:T(8,128)(2,1)}, f32[1,4,768,800]{2,3,1,0:T(8,128)}) fusion(f32[4,768]{1,0:T(4,128)S(1)} %fusion.71, f32[4,768]{1,0:T(4,128)S(1)} %get-tuple-element.293, f32[800,768,4]{1,0,2:T(8,128)S(1)} %get-tuple-element.292, pred[768,800]{0,1:T(8,128)(4,1)S(1)} %fusion.68), kind=kLoop, calls=%fused_computation.66.clone.1 | loop fusion | flops 12288000 | bytes 25214976 | tf_op jit(solution)/shard_map/while/body/eval_jaxpr/convert_element_type | solution.py:54
  116.7 3.5 multiply_reduce_fusion.2
  137.3 6.2 %fusion.72 = (bf16[1,4,768,800]{2,3,1,0:T(8,128)(2,1)}, f32[1,4,768,800]{2,3,1,0:T(8,128)}) fusion(f32[4,768]{1,0:T(4,128)S(1)} %fusion.71, f32[4,768]{1,0:T(4,128)S(1)} %get-tuple-element.293, f32[800,768,4]{1,0,2:T(8,128)S(1)} %get-tuple-element.292, pred[768,800]{0,1:T(8,128)(4,1)S(1)} %fusion.68), kind=kLoop, calls=%fused_computation.66.clone.1 | loop fusion | flops 12288000 | bytes 25214976 | tf_op jit(solution)/shard_map/while/body/eval_jaxpr/convert_element_type | solution.py:54
  145.5 3.5 multiply_reduce_fusion.2
  166.1 6.2 %fusion.72 = (bf16[1,4,768,800]{2,3,1,0:T(8,128)(2,1)}, f32[1,4,768,800]{2,3,1,0:T(8,128)}) fusion(f32[4,768]{1,0:T(4,128)S(1)} %fusion.71, f32[4,768]{1,0:T(4,128)S(1)} %get-tuple-element.293, f32[800,768,4]{1,0,2:T(8,128)S(1)} %get-tuple-element.292, pred[768,800]{0,1:T(8,128)(4,1)S(1)} %fusion.68), kind=kLoop, calls=%fused_computation.66.clone.1 | loop fusion | flops 12288000 | bytes 25214976 | tf_op jit(solution)/shard_map/while/body/eval_jaxpr/convert_element_type | solution.py:54
  174.4 3.5 multiply_reduce_fusion.2
  195.0 6.2 %fusion.72 = (bf16[1,4,768,800]{2,3,1,0:T(8,128)(2,1)}, f32[1,4,768,800]{2,3,1,0:T(8,128)}) fusion(f32[4,768]{1,0:T(4,128)S(1)} %fusion.71, f32[4,768]{1,0:T(4,128)S(1)} %get-tuple-element.293, f32[800,768,4]{1,0,2:T(8,128)S(1)} %get-tuple-element.292, pred[768,800]{0,1:T(8,128)(4,1)S(1)} %fusion.68), kind=kLoop, calls=%fused_computation.66.clone.1 | loop fusion | flops 12288000 | bytes 25214976 | tf_op jit(solution)/shard_map/while/body/eval_jaxpr/convert_element_type | solution.py:54
  203.2 3.5 multiply_reduce_fusion.2
  223.8 6.2 %fusion.72 = (bf16[1,4,768,800]{2,3,1,0:T(8,128)(2,1)}, f32[1,4,768,800]{2,3,1,0:T(8,128)}) fusion(f32[4,768]{1,0:T(4,128)S(1)} %fusion.71, f32[4,768]{1,0:T(4,128)S(1)} %get-tuple-element.293, f32[800,768,4]{1,0,2:T(8,128)S(1)} %get-tuple-element.292, pred[768,800]{0,1:T(8,128)(4,1)S(1)} %fusion.68), kind=kLoop, calls=%fused_computation.66.clone.1 | loop fusion | flops 12288000 | bytes 25214976 | tf_op jit(solution)/shard_map/while/body/eval_jaxpr/convert_element_type | solution.py:54
  232.1 3.5 multiply_reduce_fusion.2
  252.7 6.2 %fusion.72 = (bf16[1,4,768,800]{2,3,1,0:T(8,128)(2,1)}, f32[1,4,768,800]{2,3,1,0:T(8,128)}) fusion(f32[4,768]{1,0:T(4,128)S(1)} %fusion.71, f32[4,768]{1,0:T(4,128)S(1)} %get-tuple-element.293, f32[800,768,4]{1,0,2:T(8,128)S(1)} %get-tuple-element.292, pred[768,800]{0,1:T(8,128)(4,1)S(1)} %fusion.68), kind=kLoop, calls=%fused_computation.66.clone.1 | loop fusion | flops 12288000 | bytes 25214976 | tf_op jit(solution)/shard_map/while/body/eval_jaxpr/convert_element_type | solution.py:54
  260.9 3.5 multiply_reduce_fusion.2
  270.3 9.5 %all_to_all.36 = f32[8,32,256]{2,1,0:T(8,128)S(1)} all-to-all(f32[8,32,256]{2,1,0:T(8,128)} %get-tuple-element.118), channel_id=1, replica_groups=mesh['dp'=16,'tensor'=8] {'tensor'}, dimensions={0} | all-to-all | bytes 524288 | tf_op jit(solution)/shard_map/all_to_all | solution.py:105
  282.9 152.3 %all-reduce.2.cloned.1.call-done = f32[256,2048]{1,0:T(8,128)} async-done(((f32[256,2048]{1,0:T(8,128)}), f32[256,2048]{1,0:T(8,128)}) %all-reduce.2.cloned.1.call-update) | async-done | bytes 2097168 | tf_op jit(solution)/shard_map/psum | solution.py:114
  435.3 3.1 broadcast_multiply_fusion
  (208 shorter events, 161.8 us)
Async XLA Ops:
  7.2 3.7 copy-start
  7.2 32.3 %copy-start.2 = (s32[8]{0:T(128)S(1)}, s32[8]{0:T(128)}, u32[]{:S(2)}) copy-start(s32[8]{0:T(128)} %param.21) | copy-start | bytes 100
  25.9 11.7 %all-to-all-start = ((bf16[8,2,4096]{2,1,0:T(2,128)(2,1)}), bf16[8,2,4096]{2,1,0:T(2,128)(2,1)S(1)}, u32[]{:S(2)}, u32[]{:S(2)}) async-start(bf16[8,2,4096]{2,1,0:T(2,128)(2,1)} %reshape.288), calls=%async_computation | async-start | bytes 262144 | tf_op jit(solution)/shard_map/all_to_all | solution.py:95
  32.1 403.2 %all-reduce.2.cloned.1.call-start = ((), (), s32[]{:S(2)}) async-start(), calls=%async_computation.2 | async-start | bytes 4194304 | tf_op jit(solution)/shard_map/psum | solution.py:114
  39.5 240.3 %copy-start.1 = (bf16[32,256]{1,0:T(8,128)(2,1)S(1)}, bf16[32,256]{1,0:T(8,128)(2,1)}, u32[]{:S(2)}) copy-start(bf16[32,256]{1,0:T(8,128)(2,1)} %param.15) | copy-start | bytes 49156
Sparse Core Ops, SparseCore 0:
  282.3 152.8 all-reduce.1
where the time goes:
time: 448 us; the launch traced here: 445 us
  waiting for transfers between devices  158 us (35%)
  other arithmetic  108 us (24%)
  local copies, waits for them, and re-layouts  77.2 us (17%)
  matrix products  71.9 us (16%)
  between operations  14.1 us (3%)
  blocking collectives  9.49 us (2%)
  starting transfers between devices  6.42 us (1%)
    psum x1, waiting for transfers between devices, shards(): weight_grad = lax.psum(partial_grad, ('dp', 'tensor')) / example_count  152 us
    convert_element_type x8, other arithmetic, attend(): weights = probs.astype(jnp.bfloat16)  49.7 us
    dynamic_slice x40, local copies, waits for them, and re-layouts, shards(): lax.map(one_sequence, (query_own, key_own, value_own, prefix, out_grad, s...  42.8 us
    dot_general x8, matrix products, attend(): jnp.einsum('kgij,jkd->ikgd', weights, all_values, preferred_element_type=...  28.4 us
    reduce_sum x8, other arithmetic, attend(): probs = exp_scores / jnp.sum(exp_scores, axis=-1, keepdims=True)  17 us
    dot_general x8, matrix products, attend(): jnp.einsum('ikgd,jkd->kgij', query_heads, all_keys, preferred_element_typ...  14.7 us
    dynamic_update_slice x24, local copies, waits for them, and re-layouts, shards(): lax.map(one_sequence, (query_own, key_own, value_own, prefix, out_grad, s...  14.7 us
    reshape x8, local copies, waits for them, and re-layouts, attend(): key_own.reshape(row_count, shared_heads, HD)  13.9 us
  transfers between devices with their start and end apart: 2, of which 2 were waited for; matrix products, arithmetic and copies ran while one was open for 0% of the time, Pallas kernels for 0%

commit v1 on v0

v1 whole, which is shorter than its diff:
```python
import functools
import jax
import jax.numpy as jnp
from jax import lax
from jax.experimental import pallas as pl
from jax.experimental.pallas import tpu as pltpu
from jax.sharding import PartitionSpec as P

HD = 128
F32 = jnp.float32
BF16 = jnp.bfloat16
LOG2E = 1.4426950408889634
NT = (((1,), (1,)), ((), ()))
TN = (((0,), (0,)), ((), ()))
MESH = pl.DeviceIdType.MESH


def dot(a, b, dims=(((1,), (0,)), ((), ()))):
    return lax.dot_general(a, b, dims, preferred_element_type=F32)


def encode_kernel(n, ids_hbm, amt_hbm, table_hbm, pos_hbm, weight_hbm, prefix_ref, hidden_ref,
                  ids_ref, amt_ref, table_ref, pos_ref, wbuf, mine, got, send_sem, recv_sem, load_sem):
    d, t = lax.axis_index("dp"), lax.axis_index("tensor")
    barrier = pltpu.get_barrier_semaphore()
    for i in range(1, n):
        pl.semaphore_signal(barrier, inc=1, device_id=(d, lax.rem(t + i, n)), device_id_type=MESH)
    cols = wbuf.shape[1]
    loads = [pltpu.make_async_copy(src, dst, load_sem.at[i]) for i, (src, dst) in enumerate((
        (ids_hbm, ids_ref), (amt_hbm, amt_ref), (table_hbm, table_ref), (pos_hbm, pos_ref),
        (weight_hbm.at[:, pl.ds(pl.multiple_of(t * cols, cols), cols)], wbuf)))]
    for load in loads:
        load.start()
    loads[0].wait()
    loads[1].wait()
    tags = table_ref.shape[0]
    lane = lax.broadcasted_iota(jnp.int32, (1, tags), 1)
    ids, amounts = ids_ref[...], amt_ref[...]
    mix = jnp.zeros((1, tags), F32)
    for k in range(ids.shape[1]):
        mix += jnp.where(ids[:, k:k + 1] == lane, amounts[:, k:k + 1], 0.0)
    mix = mix / jnp.sum(amounts, axis=1, keepdims=True)
    mine[...] = jnp.broadcast_to(mix, mine.shape)
    got[t] = jnp.broadcast_to(mix, mine.shape)
    pl.semaphore_wait(barrier, n - 1)
    copies = []
    for i in range(1, n):
        copy = pltpu.make_async_remote_copy(
            src_ref=mine, dst_ref=got.at[t], send_sem=send_sem.at[i], recv_sem=recv_sem.at[i],
            device_id=(d, lax.rem(t + i, n)), device_id_type=MESH)
        copy.start()
        copies.append(copy)
    for load in loads[2:]:
        load.wait()
    for copy in copies:
        copy.wait()
    mixture = jnp.concatenate([got[j, 0:1] for j in range(n)], 0)
    pooled = jnp.dot(mixture, table_ref[...].astype(F32), precision=lax.Precision.HIGHEST,
                     preferred_element_type=F32)
    pos = pos_ref[...].astype(F32)
    hidden = jnp.concatenate([jnp.tanh(pos + pooled[j:j + 1]) for j in range(n)], 0).astype(BF16)
    hidden_ref[...] = hidden
    prefix_ref[...] = dot(hidden, wbuf[...]).astype(BF16).reshape(prefix_ref.shape)


def encode(tag_ids, tag_amounts, tag_table, position_table, prefix_weight):
    n = lax.axis_size("tensor")
    width, total = prefix_weight.shape
    plen = position_table.shape[0]
    vmem = pl.BlockSpec(memory_space=pltpu.VMEM)
    return pl.pallas_call(
        functools.partial(encode_kernel, n),
        out_shape=(jax.ShapeDtypeStruct((n, plen, total // n), BF16),
                   jax.ShapeDtypeStruct((n * plen, width), BF16)),
        in_specs=[pl.BlockSpec(memory_space=pltpu.HBM)] * 5,
        out_specs=(vmem, vmem),
        scratch_shapes=[
            pltpu.VMEM(tag_ids.shape, jnp.int32),
            pltpu.VMEM(tag_amounts.shape, F32),
            pltpu.VMEM(tag_table.shape, BF16),
            pltpu.VMEM(position_table.shape, BF16),
            pltpu.VMEM((width, total // n), BF16),
            pltpu.VMEM((8, tag_table.shape[0]), F32),
            pltpu.VMEM((n, 8, tag_table.shape[0]), F32),
            pltpu.SemaphoreType.DMA((n,)),
            pltpu.SemaphoreType.DMA((n,)),
            pltpu.SemaphoreType.DMA((5,)),
        ],
        compiler_params=pltpu.CompilerParams(collective_id=0, has_side_effects=True, vmem_limit_bytes=56 * 1024 * 1024),
    )(tag_ids, tag_amounts, tag_table, position_table, prefix_weight)


def attend_kernel(NR, len_ref, q_ref, k_ref, v_ref, g_ref, pre_ref, out_ref, pg_ref,
                  vx, pkbd, pvbd, ds_scr, w_scr, pp_scr, bad_scr):
    step = pl.program_id(0)
    length = len_ref[step]
    rows = q_ref.shape[1]
    heads = q_ref.shape[2] // HD
    plen = pre_ref.shape[1]
    seg_w = heads * plen
    scale = 1.0 / HD**0.5

    @pl.when(step == 0)
    def _():
        pkbd[...] = jnp.zeros_like(pkbd)
        pvbd[...] = jnp.zeros_like(pvbd)
        for h in range(heads):
            pvbd[h * plen:(h + 1) * plen, (heads + h) * HD:(heads + h + 1) * HD] = jnp.full((plen, HD), -1.0, BF16)
        vx[0:seg_w, HD:] = jnp.ones((seg_w, HD), BF16)

    pk = pre_ref[0, :, :HD]
    pv = pre_ref[0, :, HD:]
    for h in range(heads):
        pkbd[h * plen:(h + 1) * plen, h * HD:(h + 1) * HD] = pk
        pvbd[h * plen:(h + 1) * plen, h * HD:(h + 1) * HD] = pv
        vx[h * plen:(h + 1) * plen, :HD] = pv
    live = lax.broadcasted_iota(jnp.int32, (rows, HD), 0) < length
    vx[seg_w:, :HD] = jnp.where(live, v_ref[0].astype(F32), 0.0).astype(BF16)
    vx[seg_w:, HD:] = jnp.where(live, 1.0, 0.0).astype(BF16)

    seg = lax.broadcasted_iota(jnp.int32, (NR, seg_w), 1) // plen
    causal = (lax.broadcasted_iota(jnp.int32, (heads * NR, NR), 1)
              <= lax.broadcasted_iota(jnp.int32, (heads * NR, NR), 0) % NR)
    c = scale * LOG2E

    def grads(r0, nr, probs, g, out):
        go = (g.astype(F32) * out.astype(F32)).astype(BF16)
        diff = dot(g, pvbd[:, :heads * HD], NT) + dot(go, pvbd[:, heads * HD:], NT)
        alive = lax.broadcasted_iota(jnp.int32, (nr, seg_w), 0) + r0 < length
        ds_scr[pl.ds(r0, nr)] = jnp.where(alive, probs * diff, 0.0).astype(BF16)
        w_scr[pl.ds(r0, nr)] = jnp.where(alive, probs, 0.0).astype(BF16)

    def finish():
        dk = dot(ds_scr[...], q_ref[0], TN)
        dv = dot(w_scr[...], g_ref[0], TN)
        pg_ref[0, :, :HD] = sum(dk[h * plen:(h + 1) * plen, h * HD:(h + 1) * HD] for h in range(heads)) * scale
        pg_ref[0, :, HD:] = sum(dv[h * plen:(h + 1) * plen, h * HD:(h + 1) * HD] for h in range(heads))

    bad = jnp.zeros((8, HD), F32)
    for r0 in range(0, rows, NR):
        qr = q_ref[0, r0:r0 + NR]
        q4 = jnp.concatenate([qr[:, h * HD:(h + 1) * HD] for h in range(heads)], 0)
        pp = jnp.exp2(dot(qr, pkbd[...], NT) * c)
        ppb = pp.astype(BF16)
        zero = jnp.zeros_like(ppb)
        parts = [jnp.concatenate([jnp.where(seg == h, ppb, zero) for h in range(heads)], 0)]
        if r0:
            parts.append(jnp.exp2(dot(q4, k_ref[0, :r0], NT) * c).astype(BF16))
        diag = jnp.exp2(dot(q4, k_ref[0, r0:r0 + NR], NT) * c)
        parts.append(jnp.where(causal, diag, 0.0).astype(BF16))
        p = jnp.concatenate(parts, 1)
        o = dot(p, vx[:seg_w + r0 + NR])
        sums = o[:, HD:]
        ok = (sums > 1e-25) & (sums < 1e25)
        bad = jnp.maximum(bad, jnp.max(jnp.where(ok, 0.0, 1.0).reshape(-1, 8, HD), axis=0))
        inv = 1.0 / sums
        o = (o[:, :HD] * inv).astype(BF16)
        inv_seg = inv[:NR]
        for h in range(1, heads):
            inv_seg = jnp.where(seg == h, inv[h * NR:(h + 1) * NR], inv_seg)
        out = jnp.concatenate([o[h * NR:(h + 1) * NR] for h in range(heads)], 1)
        out_ref[0, r0:r0 + NR] = out
        grads(r0, NR, pp * inv_seg, g_ref[0, r0:r0 + NR], out)
    finish()

    @pl.when(jnp.max(bad) > 0.0)
    def _():
        nr = HD
        seg1 = lax.broadcasted_iota(jnp.int32, (nr, seg_w), 1) // plen

        def block(r, carry):
            r0 = pl.multiple_of(r * nr, nr)
            sp_all = dot(q_ref[0, pl.ds(r0, nr)], pkbd[...], NT) * scale
            row = lax.broadcasted_iota(jnp.int32, (nr, rows), 0) + r0
            col = lax.broadcasted_iota(jnp.int32, (nr, rows), 1)
            seen = (col <= row) & (col < length)
            pp_scr[...] = jnp.zeros_like(pp_scr)

            def head(h, carry):
                lanes = pl.ds(pl.multiple_of(h * HD, HD), HD)
                s = dot(q_ref[0, pl.ds(r0, nr), lanes], k_ref[0], NT) * scale
                s = jnp.where(seen, s, -1e30)
                sp = jnp.where(seg1 == h, sp_all, -1e30)
                m = jnp.maximum(jnp.max(s, axis=1, keepdims=True), jnp.max(sp, axis=1, keepdims=True))
                p = jnp.exp(s - m)
                p_pre = jnp.exp(sp - m)
                inv = 1.0 / (jnp.sum(p, axis=1, keepdims=True) + jnp.sum(p_pre, axis=1, keepdims=True))
                p_pre = p_pre * inv
                o = (dot((p * inv).astype(BF16), vx[seg_w:, :HD])
                     + dot(p_pre.astype(BF16), vx[:seg_w, :HD]))
                out_ref[0, pl.ds(r0, nr), lanes] = o.astype(BF16)
                pp_scr[...] += p_pre
                return carry

            lax.fori_loop(0, heads, head, 0)
            grads(r0, nr, pp_scr[...], g_ref[0, pl.ds(r0, nr)], out_ref[0, pl.ds(r0, nr)])
            return carry

        lax.fori_loop(0, rows // nr, block, 0)
        finish()


def attention(lengths, q, k, v, g, prefix, NR=256):
    n, rows, width = q.shape
    heads = width // HD
    plen = prefix.shape[1]
    seg_w = heads * plen
    spec = lambda shape: pl.BlockSpec((1,) + shape, lambda e: (e, 0, 0))
    return pl.pallas_call(
        functools.partial(attend_kernel, NR),
        grid=(n,),
        out_shape=(jax.ShapeDtypeStruct(q.shape, BF16), jax.ShapeDtypeStruct((n, plen, 2 * HD), F32)),
        in_specs=[pl.BlockSpec(memory_space=pltpu.SMEM), spec((rows, width)), spec((rows, HD)), spec((rows, HD)),
                  spec((rows, width)), spec((plen, 2 * HD))],
        out_specs=(spec((rows, width)), spec((plen, 2 * HD))),
        scratch_shapes=[
            pltpu.VMEM((seg_w + rows, 2 * HD), BF16),
            pltpu.VMEM((seg_w, width), BF16),
            pltpu.VMEM((seg_w, 2 * width), BF16),
            pltpu.VMEM((rows, seg_w), BF16),
            pltpu.VMEM((rows, seg_w), BF16),
            pltpu.VMEM((HD, seg_w), F32),
            pltpu.VMEM((8, HD), F32),
        ],
        compiler_params=pltpu.CompilerParams(vmem_limit_bytes=56 * 1024 * 1024),
    )(lengths, q, k, v, g, prefix)


def exchange_kernel(hidden_ref, pg_ref, own_ref, all_ref,
                    out_buf, part, landed, sems_pg, sems_rs, sems_ag):
    d, t = lax.axis_index("dp"), lax.axis_index("tensor")
    y, zh, core = d // 4, lax.rem(d // 2, 2), lax.rem(d, 2)
    zl, x = t // 4, lax.rem(t, 4)
    z = zh * 2 + zl

    def device(x, y, z, core):
        return ((y * 2 + z // 2) * 2 + core, lax.rem(z, 2) * 4 + x)

    barrier = pltpu.get_barrier_semaphore()
    nt, nd = 8, 16
    peers = [(d, lax.rem(t + i, nt)) for i in range(1, nt)]
    peers += [(lax.rem(d + i, nd), t) for i in range(1, nd)]
    peers += [device(x, y, lax.rem(z + i, 4), core) for i in range(1, 4)]
    for peer in peers:
        pl.semaphore_signal(barrier, inc=1, device_id=peer, device_id_type=MESH)

    pg = pg_ref[...]
    high = pg.astype(BF16)
    out_buf[...] = high
    flat = pg.reshape(-1, pg.shape[2])
    flat_high = high.reshape(flat.shape)
    low = (flat - flat_high.astype(F32)).astype(BF16)
    hidden = hidden_ref[...]
    total = dot(hidden, flat_high, TN) + dot(hidden, low, TN)
    part[...] = total.astype(BF16).reshape(part.shape)
    own_ref[t] = out_buf[t]
    pl.semaphore_wait(barrier, len(peers))

    def send(src, dst, sems, i, peer):
        copy = pltpu.make_async_remote_copy(
            src_ref=src, dst_ref=dst, send_sem=sems.at[0, i], recv_sem=sems.at[1, i],
            device_id=peer, device_id_type=MESH)
        copy.start()
        return copy

    rs = []
    for i in range(1, nd):
        to = lax.rem(d + i, nd)
        rs.append(send(part.at[to], landed.at[i], sems_rs, i, (to, t)))
    a2a = []
    for i in range(1, nt):
        to = lax.rem(t + i, nt)
        a2a.append(send(out_buf.at[to], own_ref.at[t], sems_pg, i, (d, to)))
    chunk = part[d].astype(F32)
    for i, copy in enumerate(rs):
        copy.wait()
        chunk += landed[i + 1].astype(F32)
    all_ref[core, z, y, x] = (chunk * (1.0 / 128)).astype(BF16)
    pending = []
    for phase, (block, peer) in enumerate((
            (all_ref.at[core, z, y, x], lambda i: device(lax.rem(x + i, 4), y, z, core)),
            (all_ref.at[core, z, y], lambda i: device(x, lax.rem(y + i, 4), z, core)),
            (all_ref.at[core, z], lambda i: device(x, y, lax.rem(z + i, 4), core)))):
        copies = [send(block, block, sems_ag, phase * 4 + i, peer(i)) for i in range(1, 4)]
        for copy in copies:
            copy.wait()
    last = send(all_ref.at[core], all_ref.at[core], sems_ag, 0, device(x, y, z, 1 - core))
    last.wait()
    for copy in a2a:
        copy.wait()


def exchange(hidden, pgrads):
    n, plen, cols = pgrads.shape
    width = hidden.shape[1]
    nd = 16
    vmem = pl.BlockSpec(memory_space=pltpu.VMEM)
    return pl.pallas_call(
        exchange_kernel,
        out_shape=(jax.ShapeDtypeStruct((n, plen, cols), BF16),
                   jax.ShapeDtypeStruct((2, 4, 4, 4, width // nd, cols), BF16)),
        in_specs=[vmem, vmem],
        out_specs=(vmem, vmem),
        scratch_shapes=[
            pltpu.VMEM((n, plen, cols), BF16),
            pltpu.VMEM((nd, width // nd, cols), BF16),
            pltpu.VMEM((nd, width // nd, cols), BF16),
            pltpu.SemaphoreType.DMA((2, n)),
            pltpu.SemaphoreType.DMA((2, nd)),
            pltpu.SemaphoreType.DMA((2, 12)),
        ],
        compiler_params=pltpu.CompilerParams(collective_id=1, has_side_effects=True, vmem_limit_bytes=56 * 1024 * 1024),
    )(hidden, pgrads)


def finish_kernel(own_ref, all_ref, prefix_grad_ref, weight_grad_ref):
    cols = own_ref.shape[2]
    for j in range(own_ref.shape[0]):
        prefix_grad_ref[0, :, j * cols:(j + 1) * cols] = own_ref[j].astype(F32)
    rows = all_ref.shape[4]
    for core in range(2):
        for z in range(4):
            r0 = ((z // 2) * 2 + core) * rows
            for x in range(4):
                c0 = ((z % 2) * 4 + x) * cols
                weight_grad_ref[r0:r0 + rows, c0:c0 + cols] = all_ref[core, z, 0, x].astype(F32)


def finish(own, gathered):
    n, plen, cols = own.shape
    rows = gathered.shape[4]
    return pl.pallas_call(
        finish_kernel,
        grid=(4,),
        out_shape=(jax.ShapeDtypeStruct((1, plen, n * cols), F32),
                   jax.ShapeDtypeStruct((16 * rows, n * cols), F32)),
        in_specs=[pl.BlockSpec((n // 4, plen, cols), lambda y: (y, 0, 0)),
                  pl.BlockSpec((2, 4, 1, 4, rows, cols), lambda y: (0, 0, y, 0, 0, 0))],
        out_specs=(pl.BlockSpec((1, plen, n // 4 * cols), lambda y: (0, 0, y)),
                   pl.BlockSpec((4 * rows, n * cols), lambda y: (y, 0))),
        compiler_params=pltpu.CompilerParams(vmem_limit_bytes=56 * 1024 * 1024),
    )(own, gathered)


def shards(tag_ids, tag_amounts, tag_table, position_table, prefix_weight,
           query_own, key_own, value_own, out_grad, seq_lengths):
    prefix, hidden = encode(tag_ids, tag_amounts, tag_table, position_table, prefix_weight)
    attn_out, pgrads = attention(seq_lengths, query_own, key_own, value_own, out_grad, prefix)
    prefix_grad, weight_grad = finish(*exchange(hidden, pgrads))
    return attn_out, prefix_grad, weight_grad


def solution(mesh):
    return jax.shard_map(
        shards,
        mesh=mesh,
        in_specs=(
            P(("dp", "tensor"), None),
            P(("dp", "tensor"), None),
            P(),
            P(),
            P(),
            P("dp", None, "tensor"),
            P("dp", None, "tensor"),
            P("dp", None, "tensor"),
            P("dp", None, "tensor"),
            P("dp"),
        ),
        out_specs=(P("dp", None, "tensor"), P(("dp", "tensor"), None, None), P()),
        check_vma=False,
    )
```

time: 448 us -> 232 us (0.52)
  Pallas kernels: 0 us -> 231 us
  waiting for transfers between devices: 158 us -> 0 us
  other arithmetic: 108 us -> 0 us
  local copies, waits for them, and re-layouts: 77.2 us -> 0 us
  matrix products: 71.9 us -> 0 us
  between operations: 14.1 us -> 0.65 us
  blocking collectives: 9.49 us -> 0 us
  starting transfers between devices: 6.42 us -> 0 us
    pallas_call x0 -> x4, Pallas kernels: none -> 231 us  [the longest x1 187 us: attention(): pl.pallas_call(functools.partial(attend_kernel, NR), grid=(n,), out_shape...]
    psum x1 -> x0, waiting for transfers between devices: 152 us -> none  [shards(): weight_grad = lax.psum(partial_grad, ('dp', 'tensor')) / example_count]
    dot_general x35 -> x0, matrix products: 71.9 us -> none  [the longest x8 28.4 us: attend(): jnp.einsum('kgij,jkd->ikgd', weights, all_values, preferred_element_type=...]
    convert_element_type x8 -> x0, other arithmetic: 49.7 us -> none  [attend(): weights = probs.astype(jnp.bfloat16)]
    dynamic_slice x40 -> x0, local copies, waits for them, and re-layouts: 42.8 us -> none  [shards(): lax.map(one_sequence, (query_own, key_own, value_own, prefix, out_grad, s...]
    reduce_sum x10 -> x0, other arithmetic: 19.1 us -> none  [the longest x8 17 us: attend(): probs = exp_scores / jnp.sum(exp_scores, axis=-1, keepdims=True)]
    reshape x17 -> x0, local copies, waits for them, and re-layouts: 14.7 us -> none  [the longest x8 13.9 us: attend(): key_own.reshape(row_count, shared_heads, HD)]
    dynamic_update_slice x24 -> x0, local copies, waits for them, and re-layouts: 14.7 us -> none  [shards(): lax.map(one_sequence, (query_own, key_own, value_own, prefix, out_grad, s...]
  transfers between devices with their start and end apart: 2 -> 0, of which waited for: 2 -> 0; matrix products, arithmetic and copies ran while one was open for 0% -> 0% of each run, Pallas kernels for 0% -> 0%
where the time goes in v1:
time: 232 us
  Pallas kernels  231 us (100%)
    pallas_call x1, Pallas kernels, attention(): pl.pallas_call(functools.partial(attend_kernel, NR), grid=(n,), out_shape...  187 us
    pallas_call x1, Pallas kernels, exchange(): pl.pallas_call(exchange_kernel, out_shape=(jax.ShapeDtypeStruct((n, plen,...  32.2 us
    pallas_call x1, Pallas kernels, encode(): pl.pallas_call(functools.partial(encode_kernel, n), out_shape=(jax.ShapeD...  8.32 us

profile of v1, /device:TPU:1, one launch (start us, length us, event | category | flops | bytes accessed | tf_op | source)
XLA Modules:
  0.0 231.9 jit_solution(4959993807816713002)
XLA Ops:
  0.6 8.3 %shard_map.121 = (bf16[8,32,256]{2,1,0:T(8,128)(2,1)}, bf16[256,256]{1,0:T(8,128)(2,1)}) custom-call(s32[1,8]{1,0:T(1,128)} %ids_hbm.1, f32[1,8]{1,0:T(1,128)} %amt_hbm.1, bf16[128,256]{1,0:T(8,128)(2,1)} %table_hbm.1, bf16[32,256]{1,0:T(8,128)(2,1)} %pos_hbm.1, bf16[256,2048]{1,0:T(8,128)(2,1)} %weight_hbm.1), custom_call_target="tpu_custom_call" | custom-call | tf_op jit(solution)/shard_map/pallas_call | solution.py:71
  9.0 187.1 %shard_map.122 = (bf16[8,768,512]{2,1,0:T(8,128)(2,1)}, f32[8,32,256]{2,1,0:T(8,128)}) custom-call(s32[8]{0:T(128)} %len_ref.1, bf16[8,768,512]{2,1,0:T(8,128)(2,1)} %q_ref.1, bf16[8,768,128]{2,1,0:T(8,128)(2,1)} %k_ref.1, bf16[8,768,128]{2,1,0:T(8,128)(2,1)} %v_ref.1, bf16[8,768,512]{2,1,0:T(8,128)(2,1)} %g_ref.1, bf16[8,32,256]{2,1,0:T(8,128)(2,1)} %get-tuple-element.11.pre_ref), custom_call_target="tpu_custom_call" | custom-call | tf_op jit(solution)/shard_map/pallas_call | solution.py:209
  196.1 32.2 %shard_map.123 = (bf16[8,32,256]{2,1,0:T(8,128)(2,1)}, bf16[2,4,4,4,16,256]{5,4,3,2,1,0:T(8,128)(2,1)}) custom-call(bf16[256,256]{1,0:T(8,128)(2,1)} %get-tuple-element.13.hidden_ref, f32[8,32,256]{2,1,0:T(8,128)} %get-tuple-element.14.pg_ref), custom_call_target="tpu_custom_call" | custom-call | tf_op jit(solution)/shard_map/pallas_call | solution.py:298
  228.2 3.7 %shard_map.124 = (f32[1,32,2048]{2,1,0:T(8,128)}, f32[256,2048]{1,0:T(8,128)}) custom-call(bf16[8,32,256]{2,1,0:T(8,128)(2,1)} %get-tuple-element.15.own_ref, bf16[2,4,4,4,16,256]{5,4,3,2,1,0:T(8,128)(2,1)} %get-tuple-element.16.all_ref), custom_call_target="tpu_custom_call" | custom-call | tf_op jit(solution)/shard_map/pallas_call | solution.py:332

commit v2 on v1

v2 whole, which is shorter than its diff:
```python
import functools
import jax
import jax.numpy as jnp
from jax import lax
from jax.experimental import pallas as pl
from jax.experimental.pallas import tpu as pltpu
from jax.sharding import PartitionSpec as P

HD = 128
SEQS = 128
F32 = jnp.float32
BF16 = jnp.bfloat16
LOG2E = 1.4426950408889634
NT = (((1,), (1,)), ((), ()))
TN = (((0,), (0,)), ((), ()))
MESH = pl.DeviceIdType.MESH


def dot(a, b, dims=(((1,), (0,)), ((), ()))):
    return lax.dot_general(a, b, dims, preferred_element_type=F32)


def encode_kernel(n, ids_hbm, amt_hbm, table_hbm, pos_hbm, weight_hbm, prefix_ref, hidden_ref,
                  ids_ref, amt_ref, table_ref, pos_ref, wbuf, mine, got, send_sem, recv_sem, load_sem):
    d, t = lax.axis_index("dp"), lax.axis_index("tensor")
    barrier = pltpu.get_barrier_semaphore()
    for i in range(1, n):
        pl.semaphore_signal(barrier, inc=1, device_id=(d, lax.rem(t + i, n)), device_id_type=MESH)
    cols = wbuf.shape[1]
    loads = [pltpu.make_async_copy(src, dst, load_sem.at[i]) for i, (src, dst) in enumerate((
        (ids_hbm, ids_ref), (amt_hbm, amt_ref), (table_hbm, table_ref), (pos_hbm, pos_ref),
        (weight_hbm.at[:, pl.ds(pl.multiple_of(t * cols, cols), cols)], wbuf)))]
    for load in loads:
        load.start()
    loads[0].wait()
    loads[1].wait()
    tags = table_ref.shape[0]
    lane = lax.broadcasted_iota(jnp.int32, (1, tags), 1)
    ids, amounts = ids_ref[...], amt_ref[...]
    mix = jnp.zeros((1, tags), F32)
    for k in range(ids.shape[1]):
        mix += jnp.where(ids[:, k:k + 1] == lane, amounts[:, k:k + 1], 0.0)
    mix = mix / jnp.sum(amounts, axis=1, keepdims=True)
    mine[...] = jnp.broadcast_to(mix, mine.shape)
    got[t] = jnp.broadcast_to(mix, mine.shape)
    pl.semaphore_wait(barrier, n - 1)
    copies = []
    for i in range(1, n):
        copy = pltpu.make_async_remote_copy(
            src_ref=mine, dst_ref=got.at[t], send_sem=send_sem.at[i], recv_sem=recv_sem.at[i],
            device_id=(d, lax.rem(t + i, n)), device_id_type=MESH)
        copy.start()
        copies.append(copy)
    for load in loads[2:]:
        load.wait()
    for copy in copies:
        copy.wait()
    mixture = jnp.concatenate([got[j, 0:1] for j in range(n)], 0)
    pooled = jnp.dot(mixture, table_ref[...].astype(F32), precision=lax.Precision.HIGHEST,
                     preferred_element_type=F32)
    pos = pos_ref[...].astype(F32)
    hidden = jnp.concatenate([jnp.tanh(pos + pooled[j:j + 1]) for j in range(n)], 0).astype(BF16)
    hidden_ref[...] = hidden
    prefix_ref[...] = dot(hidden, wbuf[...]).astype(BF16).reshape(prefix_ref.shape)


def encode(tag_ids, tag_amounts, tag_table, position_table, prefix_weight):
    n = lax.axis_size("tensor")
    width, total = prefix_weight.shape
    plen = position_table.shape[0]
    vmem = pl.BlockSpec(memory_space=pltpu.VMEM)
    return pl.pallas_call(
        functools.partial(encode_kernel, n),
        out_shape=(jax.ShapeDtypeStruct((n, plen, total // n), BF16),
                   jax.ShapeDtypeStruct((n * plen, width), BF16)),
        in_specs=[pl.BlockSpec(memory_space=pltpu.HBM)] * 5,
        out_specs=(vmem, vmem),
        scratch_shapes=[
            pltpu.VMEM(tag_ids.shape, jnp.int32),
            pltpu.VMEM(tag_amounts.shape, F32),
            pltpu.VMEM(tag_table.shape, BF16),
            pltpu.VMEM(position_table.shape, BF16),
            pltpu.VMEM((width, total // n), BF16),
            pltpu.VMEM((8, tag_table.shape[0]), F32),
            pltpu.VMEM((n, 8, tag_table.shape[0]), F32),
            pltpu.SemaphoreType.DMA((n,)),
            pltpu.SemaphoreType.DMA((n,)),
            pltpu.SemaphoreType.DMA((5,)),
        ],
        compiler_params=pltpu.CompilerParams(collective_id=0, has_side_effects=True, vmem_limit_bytes=56 * 1024 * 1024),
        name="encode",
    )(tag_ids, tag_amounts, tag_table, position_table, prefix_weight)


def attend_kernel(NR, GROUPS, LATE, len_ref, q_ref, k_ref, v_ref, g_ref, pre_ref, out_ref, pg_ref,
                  vx, pkbd, pvbd, ds_scr, w_scr, pp_scr):
    step = pl.program_id(0)
    length = len_ref[step]
    rows = q_ref.shape[1]
    heads = q_ref.shape[2] // HD
    plen = pre_ref.shape[1]
    seg_w = heads * plen
    scale = 1.0 / HD**0.5

    @pl.when(step == 0)
    def _():
        pkbd[...] = jnp.zeros_like(pkbd)
        pvbd[...] = jnp.zeros_like(pvbd)
        vx[0:seg_w, HD:] = jnp.ones((seg_w, HD), BF16)

    pk = pre_ref[0, :, :HD]
    pv = pre_ref[0, :, HD:]
    for h in range(heads):
        pkbd[h * plen:(h + 1) * plen, h * HD:(h + 1) * HD] = pk
        pvbd[h * plen:(h + 1) * plen, h * HD:(h + 1) * HD] = pv
        vx[h * plen:(h + 1) * plen, :HD] = pv
    live = lax.broadcasted_iota(jnp.int32, (rows, HD), 0) < length
    vx[seg_w:, :HD] = jnp.where(live, v_ref[0].astype(F32), 0.0).astype(BF16)
    vx[seg_w:, HD:] = jnp.where(live, 1.0, 0.0).astype(BF16)

    seg = lax.broadcasted_iota(jnp.int32, (NR, seg_w), 1) // plen
    c = scale * LOG2E

    per = heads // GROUPS
    causal = (lax.broadcasted_iota(jnp.int32, (per * NR, NR), 1)
              <= lax.broadcasted_iota(jnp.int32, (per * NR, NR), 0) % NR)

    def score_phase(r0):
        qr = q_ref[0, r0:r0 + NR]
        pp = jnp.exp2(dot(qr, pkbd[...], NT) * c)
        ppb = pp.astype(BF16)
        zero = jnp.zeros_like(ppb)
        ps = []
        for j in range(GROUPS):
            hs = range(j * per, (j + 1) * per)
            q4 = jnp.concatenate([qr[:, h * HD:(h + 1) * HD] for h in hs], 0)
            parts = [jnp.concatenate([jnp.where(seg == h, ppb, zero) for h in hs], 0)]
            if r0:
                parts.append(jnp.exp2(dot(q4, k_ref[0, :r0], NT) * c).astype(BF16))
            diag = jnp.exp2(dot(q4, k_ref[0, r0:r0 + NR], NT) * c)
            parts.append(jnp.where(causal, diag, 0.0).astype(BF16))
            ps.append(jnp.concatenate(parts, 1))
        return pp, ps

    def value_phase(r0, pp, ps, bad):
        invs = []
        os = [dot(p, vx[:seg_w + r0 + NR]) for p in ps]
        for j, o in enumerate(os):
            sums = o[:, HD:]
            ok = (sums > 1e-25) & (sums < 1e25)
            bad = jnp.maximum(bad, jnp.max(jnp.where(ok, 0.0, 1.0).reshape(-1, 8, HD), axis=0))
            inv = 1.0 / sums
            o = (o[:, :HD] * inv).astype(BF16)
            for i in range(per):
                h = j * per + i
                invs.append(inv[i * NR:(i + 1) * NR])
                out_ref[0, r0:r0 + NR, h * HD:(h + 1) * HD] = o[i * NR:(i + 1) * NR]
        inv_seg = invs[0]
        for h in range(1, heads):
            inv_seg = jnp.where(seg == h, invs[h], inv_seg)
        probs = pp * inv_seg
        alive = lax.broadcasted_iota(jnp.int32, (NR, seg_w), 0) + r0 < length
        probs = jnp.where(alive, probs, 0.0)
        w_scr[r0:r0 + NR] = probs.astype(BF16)
        pp_scr[r0:r0 + NR] = probs
        return bad

    def row_delta(g, out, seg_r):
        delta = None
        for h in range(heads):
            lanes = slice(h * HD, (h + 1) * HD)
            total = jnp.sum(g[:, lanes].astype(F32) * out[:, lanes].astype(F32), axis=1, keepdims=True)
            delta = jnp.broadcast_to(total, seg_r.shape) if h == 0 else jnp.where(seg_r == h, total, delta)
        return delta

    def grad_phase(r0, nr, probs):
        g = g_ref[0, r0:r0 + nr]
        seg_r = lax.broadcasted_iota(jnp.int32, (nr, seg_w), 1) // plen
        delta = row_delta(g, out_ref[0, r0:r0 + nr], seg_r)
        ds_scr[r0:r0 + nr] = (probs * (dot(g, pvbd[...], NT) - delta)).astype(BF16)

    def finish():
        w = 2 * HD
        for half in range(heads // 2):
            lanes = slice(half * w, (half + 1) * w)
            dk = dot(ds_scr[...], q_ref[0, :, lanes], TN)
            dv = dot(w_scr[...], g_ref[0, :, lanes], TN)
            for i in range(2):
                h = half * 2 + i
                a = dk[h * plen:(h + 1) * plen, i * HD:(i + 1) * HD] * scale
                b = dv[h * plen:(h + 1) * plen, i * HD:(i + 1) * HD]
                if h:
                    a, b = a + pa, b + pb
                pa, pb = a, b
        pg_ref[0, :, :HD] = pa
        pg_ref[0, :, HD:] = pb

    bad = jnp.zeros((8, HD), F32)
    starts = list(range(0, rows, NR))
    state = score_phase(starts[0])
    for i, r0 in enumerate(starts):
        now = state
        if i + 1 < len(starts):
            state = score_phase(starts[i + 1])
        bad = value_phase(r0, *now, bad)
    step_rows = rows // LATE
    for r0 in range(0, rows, step_rows):
        grad_phase(r0, step_rows, pp_scr[r0:r0 + step_rows])
    finish()

    @pl.when(jnp.max(bad) > 0.0)
    def _():
        nr = HD
        seg1 = lax.broadcasted_iota(jnp.int32, (nr, seg_w), 1) // plen

        def block(r, carry):
            r0 = pl.multiple_of(r * nr, nr)
            sp_all = dot(q_ref[0, pl.ds(r0, nr)], pkbd[...], NT) * scale
            row = lax.broadcasted_iota(jnp.int32, (nr, rows), 0) + r0
            col = lax.broadcasted_iota(jnp.int32, (nr, rows), 1)
            seen = (col <= row) & (col < length)
            pp_scr[pl.ds(r0, nr)] = jnp.zeros((nr, seg_w), F32)

            def head(h, carry):
                lanes = pl.ds(pl.multiple_of(h * HD, HD), HD)
                s = dot(q_ref[0, pl.ds(r0, nr), lanes], k_ref[0], NT) * scale
                s = jnp.where(seen, s, -1e30)
                sp = jnp.where(seg1 == h, sp_all, -1e30)
                m = jnp.maximum(jnp.max(s, axis=1, keepdims=True), jnp.max(sp, axis=1, keepdims=True))
                p = jnp.exp(s - m)
                p_pre = jnp.exp(sp - m)
                inv = 1.0 / (jnp.sum(p, axis=1, keepdims=True) + jnp.sum(p_pre, axis=1, keepdims=True))
                p_pre = p_pre * inv
                o = (dot((p * inv).astype(BF16), vx[seg_w:, :HD])
                     + dot(p_pre.astype(BF16), vx[:seg_w, :HD]))
                out_ref[0, pl.ds(r0, nr), lanes] = o.astype(BF16)
                pp_scr[pl.ds(r0, nr)] += p_pre
                return carry

            lax.fori_loop(0, heads, head, 0)
            alive = lax.broadcasted_iota(jnp.int32, (nr, seg_w), 0) + r0 < length
            probs = jnp.where(alive, pp_scr[pl.ds(r0, nr)], 0.0)
            w_scr[pl.ds(r0, nr)] = probs.astype(BF16)
            g = g_ref[0, pl.ds(r0, nr)]
            delta = row_delta(g, out_ref[0, pl.ds(r0, nr)], seg1)
            ds_scr[pl.ds(r0, nr)] = (probs * (dot(g, pvbd[...], NT) - delta)).astype(BF16)
            return carry

        lax.fori_loop(0, rows // nr, block, 0)
        finish()


def attention(lengths, q, k, v, g, prefix, NR=128, GROUPS=2, LATE=2):
    n, rows, width = q.shape
    heads = width // HD
    plen = prefix.shape[1]
    seg_w = heads * plen
    spec = lambda shape: pl.BlockSpec((1,) + shape, lambda e: (e, 0, 0))
    return pl.pallas_call(
        functools.partial(attend_kernel, NR, GROUPS, LATE),
        grid=(n,),
        out_shape=(jax.ShapeDtypeStruct(q.shape, BF16), jax.ShapeDtypeStruct((n, plen, 2 * HD), F32)),
        in_specs=[pl.BlockSpec(memory_space=pltpu.SMEM), spec((rows, width)), spec((rows, HD)), spec((rows, HD)),
                  spec((rows, width)), spec((plen, 2 * HD))],
        out_specs=(spec((rows, width)), spec((plen, 2 * HD))),
        scratch_shapes=[
            pltpu.VMEM((seg_w + rows, 2 * HD), BF16),
            pltpu.VMEM((seg_w, width), BF16),
            pltpu.VMEM((seg_w, width), BF16),
            pltpu.VMEM((rows, seg_w), BF16),
            pltpu.VMEM((rows, seg_w), BF16),
            pltpu.VMEM((rows, seg_w), F32),
        ],
        compiler_params=pltpu.CompilerParams(vmem_limit_bytes=56 * 1024 * 1024),
        name="attend",
    )(lengths, q, k, v, g, prefix)


def exchange_kernel(hid_hbm, pg_hbm, own_ref, all_ref, hid, pg, out_buf, part, landed,
                    load_sem, sems_pg, sems_rs, sems_ag, sems_core):
    d, t = lax.axis_index("dp"), lax.axis_index("tensor")
    y, zh, core = d // 4, lax.rem(d // 2, 2), lax.rem(d, 2)
    zl, x = t // 4, lax.rem(t, 4)
    z = zh * 2 + zl
    me = dict(x=x, y=y, z=z)

    def device(x, y, z, core):
        return ((y * 2 + z // 2) * 2 + core, lax.rem(z, 2) * 4 + x)

    def shifted(offsets, flip=0):
        c = {axis: lax.rem(me[axis] + offsets.get(axis, 0), 4) for axis in me}
        return device(c["x"], c["y"], c["z"], lax.rem(core + flip, 2))

    def offsets_over(axes):
        out = [{}]
        for axis in axes:
            out = [{**o, axis: i} for o in out for i in range(4)]
        far = lambda o: -sum((0, 1, 2, 1)[i] for i in o.values())
        return sorted([o for o in out if any(o.values())], key=far)

    plane, line = offsets_over("xy"), offsets_over("z")
    others = [{"y": i, "z": j} for i in (2, 1, 3, 0) for j in (2, 0) if i or j]
    sums = [(o, flip) for o in others for flip in (0, 1)] + [({}, 1)]
    tensor = [(d, lax.rem(t + i, 8)) for i in range(1, 8)]
    peers = [shifted(o) for o in plane + line]
    peers += [shifted(o, flip) for o, flip in sums if flip or (o["y"] and o["z"])]
    peers += [(d, lax.rem(zl + 1, 2) * 4 + lax.rem(x + i, 4)) for i in (1, 2, 3)]
    barrier = pltpu.get_barrier_semaphore()
    loads = [pltpu.make_async_copy(hid_hbm, hid, load_sem.at[0]),
             pltpu.make_async_copy(pg_hbm, pg, load_sem.at[1])]
    for load in loads:
        load.start()
    for peer in peers:
        pl.semaphore_signal(barrier, inc=1, device_id=peer, device_id_type=MESH)
    for load in loads:
        load.wait()
    grads = pg[...]
    high = grads.astype(BF16)
    out_buf[...] = high
    own_ref[t] = out_buf[t]
    flat_high = high.reshape(-1, high.shape[2])
    low = (grads.reshape(flat_high.shape) - flat_high.astype(F32)).astype(BF16)
    total = dot(hid[...], flat_high, TN) + dot(hid[...], low, TN)
    part[...] = total.astype(BF16).reshape(part.shape)
    pl.semaphore_wait(barrier, len(peers))

    def send(src, dst, sems, i, peer):
        copy = pltpu.make_async_remote_copy(
            src_ref=src, dst_ref=dst, send_sem=sems.at[0, i], recv_sem=sems.at[1, i],
            device_id=peer, device_id_type=MESH)
        copy.start()
        return copy

    scatter = []
    for i, (o, flip) in enumerate(sums):
        to = shifted(o, flip)
        scatter.append(send(part.at[to[0]], landed.at[i], sems_rs, i, to))
    back = [send(out_buf.at[to[1]], own_ref.at[t], sems_pg, i, to) for i, to in enumerate(tensor)]
    chunk = part[d].astype(F32)
    for i, copy in enumerate(scatter):
        copy.wait()
        chunk += landed[i].astype(F32)
    chunk = (chunk * (1.0 / SEQS)).astype(BF16)
    half = chunk.shape[1] // 2
    all_ref[0, core, z, y, x] = chunk[:, :half]
    all_ref[1, core, y, x, z] = chunk[:, half:]
    first = [send(all_ref.at[0, core, z, y, x], all_ref.at[0, core, z, y, x], sems_ag, i, shifted(o))
             for i, o in enumerate(plane)]
    first += [send(all_ref.at[1, core, y, x, z], all_ref.at[1, core, y, x, z], sems_ag, 15 + i, shifted(o))
              for i, o in enumerate(line)]
    for copy in first[15:]:
        copy.wait()
    wide = [send(all_ref.at[1, core, y, x], all_ref.at[1, core, y, x], sems_ag, 18 + i, shifted(o))
            for i, o in enumerate(plane)]
    for copy in first[:15]:
        copy.wait()
    deep = [send(all_ref.at[0, core, z], all_ref.at[0, core, z], sems_ag, 33 + i, shifted(o))
            for i, o in enumerate(line)]
    sibling = shifted({}, 1)
    passed = [send(all_ref.at[0, core, z], all_ref.at[0, core, z], sems_core, 0, sibling)]
    for o, copy in zip(line, deep):
        copy.wait()
        block = all_ref.at[0, core, lax.rem(z + 4 - o["z"], 4)]
        passed.append(send(block, block, sems_core, o["z"], sibling))
    for i in (2, 1, 3, 0):
        for o, copy in zip(plane, wide):
            if o["y"] == i:
                copy.wait()
        block = all_ref.at[1, core, lax.rem(y + 4 - i, 4)]
        passed.append(send(block, block, sems_core, 4 + i, sibling))
    for copy in passed + back:
        copy.wait()


def exchange(hidden, pgrads):
    n, plen, cols = pgrads.shape
    width = hidden.shape[1]
    rows = width // 16
    vmem = pl.BlockSpec(memory_space=pltpu.VMEM)
    return pl.pallas_call(
        exchange_kernel,
        out_shape=(jax.ShapeDtypeStruct((n, plen, cols), BF16),
                   jax.ShapeDtypeStruct((2, 2, 4, 4, 4, rows, cols // 2), BF16)),
        in_specs=[pl.BlockSpec(memory_space=pltpu.HBM)] * 2,
        out_specs=(vmem, vmem),
        scratch_shapes=[
            pltpu.VMEM(hidden.shape, BF16),
            pltpu.VMEM(pgrads.shape, F32),
            pltpu.VMEM((n, plen, cols), BF16),
            pltpu.VMEM((16, rows, cols), BF16),
            pltpu.VMEM((16, rows, cols), BF16),
            pltpu.SemaphoreType.DMA((2,)),
            pltpu.SemaphoreType.DMA((2, 8)),
            pltpu.SemaphoreType.DMA((2, 16)),
            pltpu.SemaphoreType.DMA((2, 36)),
            pltpu.SemaphoreType.DMA((2, 8)),
        ],
        compiler_params=pltpu.CompilerParams(collective_id=1, has_side_effects=True, vmem_limit_bytes=56 * 1024 * 1024),
        name="exchange",
    )(hidden, pgrads)


def finish_kernel(own_ref, first_ref, second_ref, prefix_grad_ref, weight_grad_ref):
    cols = own_ref.shape[2]
    half = cols // 2
    for j in range(own_ref.shape[0]):
        prefix_grad_ref[0, :, j * cols:(j + 1) * cols] = own_ref[j].astype(F32)
    ys, rows = first_ref.shape[3], first_ref.shape[5]
    for y in range(ys):
        for core in range(2):
            for z in range(4):
                r0 = ((y * 2 + z // 2) * 2 + core) * rows
                for x in range(4):
                    c0 = ((z % 2) * 4 + x) * cols
                    weight_grad_ref[r0:r0 + rows, c0:c0 + half] = first_ref[0, core, z, y, x].astype(F32)
                    weight_grad_ref[r0:r0 + rows, c0 + half:c0 + cols] = second_ref[0, core, y, x, z].astype(F32)


def finish(own, gathered, steps=2):
    n, plen, cols = own.shape
    rows = gathered.shape[5]
    ys = 4 // steps
    return pl.pallas_call(
        finish_kernel,
        grid=(steps,),
        out_shape=(jax.ShapeDtypeStruct((1, plen, n * cols), F32),
                   jax.ShapeDtypeStruct((16 * rows, n * cols), F32)),
        in_specs=[pl.BlockSpec((n // steps, plen, cols), lambda i: (i, 0, 0)),
                  pl.BlockSpec((1, 2, 4, ys, 4, rows, cols // 2), lambda i: (0, 0, 0, i, 0, 0, 0)),
                  pl.BlockSpec((1, 2, ys, 4, 4, rows, cols // 2), lambda i: (1, 0, i, 0, 0, 0, 0))],
        out_specs=(pl.BlockSpec((1, plen, n // steps * cols), lambda i: (0, 0, i)),
                   pl.BlockSpec((4 * ys * rows, n * cols), lambda i: (i, 0))),
        compiler_params=pltpu.CompilerParams(vmem_limit_bytes=56 * 1024 * 1024),
        name="widen",
    )(own, gathered, gathered)


def shards(tag_ids, tag_amounts, tag_table, position_table, prefix_weight,
           query_own, key_own, value_own, out_grad, seq_lengths):
    prefix, hidden = encode(tag_ids, tag_amounts, tag_table, position_table, prefix_weight)
    attn_out, pgrads = attention(seq_lengths, query_own, key_own, value_own, out_grad, prefix)
    prefix_grad, weight_grad = finish(*exchange(hidden, pgrads))
    return attn_out, prefix_grad, weight_grad


def solution(mesh):
    return jax.shard_map(
        shards,
        mesh=mesh,
        in_specs=(
            P(("dp", "tensor"), None),
            P(("dp", "tensor"), None),
            P(),
            P(),
            P(),
            P("dp", None, "tensor"),
            P("dp", None, "tensor"),
            P("dp", None, "tensor"),
            P("dp", None, "tensor"),
            P("dp"),
        ),
        out_specs=(P("dp", None, "tensor"), P(("dp", "tensor"), None, None), P()),
        check_vma=False,
    )
```

time: 232 us -> 205 us (0.88)
  Pallas kernels: 231 us -> 204 us
    pallas_call x2, Pallas kernels: 191 us -> 170 us  [the longest x1 167 us: attention(): pl.pallas_call(functools.partial(attend_kernel, NR, GROUPS, LATE), grid=(...]
    pallas_call x1, Pallas kernels: 32.2 us -> 26.5 us  [exchange(): pl.pallas_call(exchange_kernel, out_shape=(jax.ShapeDtypeStruct((n, plen,...]
where the time goes in v2:
time: 205 us
  Pallas kernels  204 us (100%)
    pallas_call x1, Pallas kernels, attention(): pl.pallas_call(functools.partial(attend_kernel, NR, GROUPS, LATE), grid=(...  167 us
    pallas_call x1, Pallas kernels, exchange(): pl.pallas_call(exchange_kernel, out_shape=(jax.ShapeDtypeStruct((n, plen,...  26.5 us
    pallas_call x1, Pallas kernels, encode(): pl.pallas_call(functools.partial(encode_kernel, n), out_shape=(jax.ShapeD...  8.32 us

profile of v2, /device:TPU:1, one launch (start us, length us, event | category | flops | bytes accessed | tf_op | source)
XLA Modules:
  0.0 205.1 jit_solution(15670968608189396461)
XLA Ops:
  0.6 8.3 %encode.1 = (bf16[8,32,256]{2,1,0:T(8,128)(2,1)}, bf16[256,256]{1,0:T(8,128)(2,1)}) custom-call(s32[1,8]{1,0:T(1,128)} %ids_hbm.1, f32[1,8]{1,0:T(1,128)} %amt_hbm.1, bf16[128,256]{1,0:T(8,128)(2,1)} %table_hbm.1, bf16[32,256]{1,0:T(8,128)(2,1)} %pos_hbm.1, bf16[256,2048]{1,0:T(8,128)(2,1)} %weight_hbm.1), custom_call_target="tpu_custom_call" | custom-call | tf_op jit(solution)/shard_map/encode/pallas_call | solution.py:72
  9.0 167.1 %attend.1 = (bf16[8,768,512]{2,1,0:T(8,128)(2,1)}, f32[8,32,256]{2,1,0:T(8,128)}) custom-call(s32[8]{0:T(128)} %len_ref.1, bf16[8,768,512]{2,1,0:T(8,128)(2,1)} %q_ref.1, bf16[8,768,128]{2,1,0:T(8,128)(2,1)} %k_ref.1, bf16[8,768,128]{2,1,0:T(8,128)(2,1)} %v_ref.1, bf16[8,768,512]{2,1,0:T(8,128)(2,1)} %g_ref.1, bf16[8,32,256]{2,1,0:T(8,128)(2,1)} %get-tuple-element.11.pre_ref), custom_call_target="tpu_custom_call" | custom-call | tf_op jit(solution)/shard_map/attend/pallas_call | solution.py:259
  176.1 26.5 %exchange.1 = (bf16[8,32,256]{2,1,0:T(8,128)(2,1)}, bf16[2,2,4,4,4,16,128]{6,5,4,3,2,1,0:T(8,128)(2,1)}) custom-call(bf16[256,256]{1,0:T(8,128)(2,1)} %get-tuple-element.13.hid_hbm, f32[8,32,256]{2,1,0:T(8,128)} %get-tuple-element.14.pg_hbm), custom_call_target="tpu_custom_call" | custom-call | tf_op jit(solution)/shard_map/exchange/pallas_call | solution.py:380
  202.6 2.5 %widen.1 = (f32[1,32,2048]{2,1,0:T(8,128)}, f32[256,2048]{1,0:T(8,128)}) custom-call(bf16[8,32,256]{2,1,0:T(8,128)(2,1)} %get-tuple-element.15.own_ref, bf16[2,2,4,4,4,16,128]{6,5,4,3,2,1,0:T(8,128)(2,1)} %get-tuple-element.16.first_ref.second_ref, bf16[2,2,4,4,4,16,128]{6,5,4,3,2,1,0:T(8,128)(2,1)} %get-tuple-element.16.first_ref.second_ref), custom_call_target="tpu_custom_call" | custom-call | tf_op jit(solution)/shard_map/widen/pallas_call | solution.py:423

commit v3 on v2

v3 whole, which is shorter than its diff:
```python
import functools
import jax
import jax.numpy as jnp
from jax import lax
from jax.experimental import pallas as pl
from jax.experimental.pallas import tpu as pltpu
from jax.sharding import PartitionSpec as P

HD = 128
SEQS = 128
F32 = jnp.float32
BF16 = jnp.bfloat16
SCALE = 1.0 / HD**0.5
LOG2E = 1.4426950408889634
NT = (((1,), (1,)), ((), ()))
TN = (((0,), (0,)), ((), ()))
MESH = pl.DeviceIdType.MESH


def dot(a, b, dims=(((1,), (0,)), ((), ()))):
    return lax.dot_general(a, b, dims, preferred_element_type=F32)


def in_hbm(*arrays):
    return [pltpu.with_memory_space_constraint(a, pltpu.HBM) for a in arrays]


def hidden_of(mixture, table, pos):
    pooled = jnp.dot(mixture, table.astype(F32), precision=lax.Precision.HIGHEST, preferred_element_type=F32)
    pos = pos.astype(F32)
    return jnp.concatenate([jnp.tanh(pos + pooled[j:j + 1]) for j in range(mixture.shape[0])], 0).astype(BF16)


def attention_scratch(rows, width, plen):
    seg_w = width // HD * plen
    return [
        pltpu.VMEM((seg_w + rows, 2 * HD), BF16),
        pltpu.VMEM((seg_w, width), BF16),
        pltpu.VMEM((seg_w, width), BF16),
        pltpu.VMEM((rows, seg_w), BF16),
        pltpu.VMEM((rows, seg_w), BF16),
        pltpu.VMEM((rows, seg_w), F32),
    ]


def clear(vx, pkbd, pvbd):
    pkbd[...] = jnp.zeros_like(pkbd)
    pvbd[...] = jnp.zeros_like(pvbd)
    seg_w = pkbd.shape[0]
    vx[0:seg_w, HD:] = jnp.ones((seg_w, HD), BF16)


def place(length, prefix, v, vx, pkbd, pvbd):
    plen, seg_w, rows = prefix.shape[0], pkbd.shape[0], v.shape[0]
    pk, pv = prefix[:, :HD], prefix[:, HD:]
    for h in range(seg_w // plen):
        pkbd[h * plen:(h + 1) * plen, h * HD:(h + 1) * HD] = pk
        pvbd[h * plen:(h + 1) * plen, h * HD:(h + 1) * HD] = pv
        vx[h * plen:(h + 1) * plen, :HD] = pv
    live = lax.broadcasted_iota(jnp.int32, (rows, HD), 0) < length
    vx[seg_w:, :HD] = jnp.where(live, v.astype(F32), 0.0).astype(BF16)
    vx[seg_w:, HD:] = jnp.where(live, 1.0, 0.0).astype(BF16)


def row_delta(g, out, plen):
    heads = g.shape[1] // HD
    seg = lax.broadcasted_iota(jnp.int32, (g.shape[0], heads * plen), 1) // plen
    delta = None
    for h in range(heads):
        lanes = slice(h * HD, (h + 1) * HD)
        total = jnp.sum(g[:, lanes].astype(F32) * out[:, lanes].astype(F32), axis=1, keepdims=True)
        delta = jnp.broadcast_to(total, seg.shape) if h == 0 else jnp.where(seg == h, total, delta)
    return delta


def prefix_gradient(q_ref, g_ref, ds_scr, w_scr, plen):
    heads = q_ref.shape[1] // HD
    for half in range(heads // 2):
        lanes = slice(half * 2 * HD, (half + 1) * 2 * HD)
        dk = dot(ds_scr[...], q_ref[:, lanes], TN)
        dv = dot(w_scr[...], g_ref[:, lanes], TN)
        for i in range(2):
            h = half * 2 + i
            a = dk[h * plen:(h + 1) * plen, i * HD:(i + 1) * HD] * SCALE
            b = dv[h * plen:(h + 1) * plen, i * HD:(i + 1) * HD]
            if h:
                a, b = a + pa, b + pb
            pa, pb = a, b
    return jnp.concatenate([pa, pb], 1)


def attend_fast(length, q_ref, k_ref, g_ref, out_ref, plen, vx, pkbd, pvbd, ds_scr, w_scr, pp_scr,
                nr=128, groups=2, late=2):
    rows, width = q_ref.shape
    heads = width // HD
    seg_w = heads * plen
    per = heads // groups
    seg = lax.broadcasted_iota(jnp.int32, (nr, seg_w), 1) // plen
    causal = (lax.broadcasted_iota(jnp.int32, (per * nr, nr), 1)
              <= lax.broadcasted_iota(jnp.int32, (per * nr, nr), 0) % nr)
    c = SCALE * LOG2E

    def score_phase(r0):
        qr = q_ref[r0:r0 + nr]
        pp = jnp.exp2(dot(qr, pkbd[...], NT) * c)
        ppb = pp.astype(BF16)
        zero = jnp.zeros_like(ppb)
        ps = []
        for j in range(groups):
            hs = range(j * per, (j + 1) * per)
            q4 = jnp.concatenate([qr[:, h * HD:(h + 1) * HD] for h in hs], 0)
            parts = [jnp.concatenate([jnp.where(seg == h, ppb, zero) for h in hs], 0)]
            if r0:
                parts.append(jnp.exp2(dot(q4, k_ref[:r0], NT) * c).astype(BF16))
            diag = jnp.exp2(dot(q4, k_ref[r0:r0 + nr], NT) * c)
            parts.append(jnp.where(causal, diag, 0.0).astype(BF16))
            ps.append(jnp.concatenate(parts, 1))
        return pp, ps

    def value_phase(r0, pp, ps, bad):
        invs = []
        os = [dot(p, vx[:seg_w + r0 + nr]) for p in ps]
        for j, o in enumerate(os):
            sums = o[:, HD:]
            ok = (sums > 1e-25) & (sums < 1e25)
            bad = jnp.maximum(bad, jnp.max(jnp.where(ok, 0.0, 1.0).reshape(-1, 8, HD), axis=0))
            inv = 1.0 / sums
            o = (o[:, :HD] * inv).astype(BF16)
            for i in range(per):
                h = j * per + i
                invs.append(inv[i * nr:(i + 1) * nr])
                out_ref[r0:r0 + nr, h * HD:(h + 1) * HD] = o[i * nr:(i + 1) * nr]
        inv_seg = invs[0]
        for h in range(1, heads):
            inv_seg = jnp.where(seg == h, invs[h], inv_seg)
        alive = lax.broadcasted_iota(jnp.int32, (nr, seg_w), 0) + r0 < length
        probs = jnp.where(alive, pp * inv_seg, 0.0)
        w_scr[r0:r0 + nr] = probs.astype(BF16)
        pp_scr[r0:r0 + nr] = probs
        return bad

    bad = jnp.zeros((8, HD), F32)
    starts = list(range(0, rows, nr))
    state = score_phase(starts[0])
    for i, r0 in enumerate(starts):
        now = state
        if i + 1 < len(starts):
            state = score_phase(starts[i + 1])
        bad = value_phase(r0, *now, bad)
    step = rows // late
    for r0 in range(0, rows, step):
        g = g_ref[r0:r0 + step]
        delta = row_delta(g, out_ref[r0:r0 + step], plen)
        ds_scr[r0:r0 + step] = (pp_scr[r0:r0 + step] * (dot(g, pvbd[...], NT) - delta)).astype(BF16)
    return prefix_gradient(q_ref, g_ref, ds_scr, w_scr, plen), bad


def attend_exact(length, q_ref, k_ref, g_ref, out_ref, plen, vx, pkbd, pvbd, ds_scr, w_scr, pp_scr):
    nr = HD
    rows, width = q_ref.shape
    heads = width // HD
    seg_w = heads * plen
    seg = lax.broadcasted_iota(jnp.int32, (nr, seg_w), 1) // plen

    def block(r, carry):
        r0 = pl.multiple_of(r * nr, nr)
        here = pl.ds(r0, nr)
        sp_all = dot(q_ref[here], pkbd[...], NT) * SCALE
        row = lax.broadcasted_iota(jnp.int32, (nr, rows), 0) + r0
        col = lax.broadcasted_iota(jnp.int32, (nr, rows), 1)
        seen = (col <= row) & (col < length)
        pp_scr[here] = jnp.zeros((nr, seg_w), F32)

        def head(h, carry):
            lanes = pl.ds(pl.multiple_of(h * HD, HD), HD)
            s = jnp.where(seen, dot(q_ref[here, lanes], k_ref[...], NT) * SCALE, -1e30)
            sp = jnp.where(seg == h, sp_all, -1e30)
            m = jnp.maximum(jnp.max(s, axis=1, keepdims=True), jnp.max(sp, axis=1, keepdims=True))
            p = jnp.exp(s - m)
            p_pre = jnp.exp(sp - m)
            inv = 1.0 / (jnp.sum(p, axis=1, keepdims=True) + jnp.sum(p_pre, axis=1, keepdims=True))
            p_pre = p_pre * inv
            o = dot((p * inv).astype(BF16), vx[seg_w:, :HD]) + dot(p_pre.astype(BF16), vx[:seg_w, :HD])
            out_ref[here, lanes] = o.astype(BF16)
            pp_scr[here] += p_pre
            return carry

        lax.fori_loop(0, heads, head, 0)
        alive = lax.broadcasted_iota(jnp.int32, (nr, seg_w), 0) + r0 < length
        probs = jnp.where(alive, pp_scr[here], 0.0)
        w_scr[here] = probs.astype(BF16)
        g = g_ref[here]
        ds_scr[here] = (probs * (dot(g, pvbd[...], NT) - row_delta(g, out_ref[here], plen))).astype(BF16)
        return carry

    lax.fori_loop(0, rows // nr, block, 0)
    return prefix_gradient(q_ref, g_ref, ds_scr, w_scr, plen)


def encode_kernel(n, len_ref, ids_hbm, amt_hbm, table_hbm, pos_hbm, weight_hbm, q_hbm, k_hbm, v_hbm, g_hbm,
                  prefix_ref, hidden_ref, out_ref, pg_ref, bad_ref, me_ref,
                  ids_ref, amt_ref, table_ref, pos_ref, wbuf, q_ref, k_ref, v_ref, g_ref, mine, got,
                  send_sem, recv_sem, load_sem, *scratch):
    d, t = lax.axis_index("dp"), lax.axis_index("tensor")
    me_ref[0] = t
    cols = wbuf.shape[1]
    loads = [pltpu.make_async_copy(src, dst, load_sem.at[i]) for i, (src, dst) in enumerate((
        (ids_hbm, ids_ref), (amt_hbm, amt_ref), (table_hbm, table_ref), (pos_hbm, pos_ref),
        (weight_hbm.at[:, pl.ds(pl.multiple_of(t * cols, cols), cols)], wbuf),
        (q_hbm.at[t], q_ref), (k_hbm.at[t], k_ref), (v_hbm.at[t], v_ref), (g_hbm.at[t], g_ref)))]
    for load in loads:
        load.start()
    barrier = pltpu.get_barrier_semaphore()
    for i in range(1, n):
        pl.semaphore_signal(barrier, inc=1, device_id=(d, lax.rem(t + i, n)), device_id_type=MESH)
    loads[0].wait()
    loads[1].wait()
    tags = table_ref.shape[0]
    lane = lax.broadcasted_iota(jnp.int32, (1, tags), 1)
    ids, amounts = ids_ref[...], amt_ref[...]
    mix = jnp.zeros((1, tags), F32)
    for k in range(ids.shape[1]):
        mix += jnp.where(ids[:, k:k + 1] == lane, amounts[:, k:k + 1], 0.0)
    mix = mix / jnp.sum(amounts, axis=1, keepdims=True)
    mine[...] = jnp.broadcast_to(mix, mine.shape)
    got[t] = jnp.broadcast_to(mix, mine.shape)
    for load in loads[2:5]:
        load.wait()
    plen = pos_ref.shape[0]
    vx, pkbd, pvbd, ds_scr, w_scr, pp_scr = scratch
    length = len_ref[t]
    clear(vx, pkbd, pvbd)
    own = dot(hidden_of(mix, table_ref[...], pos_ref[...]), wbuf[...]).astype(BF16)
    pl.semaphore_wait(barrier, n - 1)
    copies = []
    for i in range(1, n):
        copy = pltpu.make_async_remote_copy(
            src_ref=mine, dst_ref=got.at[t], send_sem=send_sem.at[i], recv_sem=recv_sem.at[i],
            device_id=(d, lax.rem(t + i, n)), device_id_type=MESH)
        copy.start()
        copies.append(copy)
    for load in loads[5:]:
        load.wait()
    place(length, own, v_ref[...], vx, pkbd, pvbd)
    pg_ref[...], bad_ref[...] = attend_fast(length, q_ref, k_ref, g_ref, out_ref, plen, *scratch)
    for copy in copies:
        copy.wait()
    mixture = jnp.concatenate([got[j, 0:1] for j in range(n)], 0)
    hidden = hidden_of(mixture, table_ref[...], pos_ref[...])
    hidden_ref[...] = hidden
    prefix_ref[...] = dot(hidden, wbuf[...]).astype(BF16).reshape(prefix_ref.shape)


def encode(lengths, tag_ids, tag_amounts, tag_table, position_table, prefix_weight, q, k, v, g):
    n, rows, width = q.shape
    units, total = prefix_weight.shape
    plen = position_table.shape[0]
    cols = total // n
    vmem = pl.BlockSpec(memory_space=pltpu.VMEM)
    smem = pl.BlockSpec(memory_space=pltpu.SMEM)
    return pl.pallas_call(
        functools.partial(encode_kernel, n),
        out_shape=(pltpu.VMEM((n, plen, cols), BF16), pltpu.VMEM((n * plen, units), BF16),
                   pltpu.VMEM((rows, width), BF16), pltpu.VMEM((plen, cols), F32),
                   pltpu.VMEM((8, HD), F32), jax.ShapeDtypeStruct((1,), jnp.int32)),
        in_specs=[smem] + [pl.BlockSpec(memory_space=pltpu.HBM)] * 9,
        out_specs=(vmem,) * 5 + (smem,),
        scratch_shapes=[
            pltpu.VMEM(tag_ids.shape, jnp.int32),
            pltpu.VMEM(tag_amounts.shape, F32),
            pltpu.VMEM(tag_table.shape, BF16),
            pltpu.VMEM(position_table.shape, BF16),
            pltpu.VMEM((units, cols), BF16),
            pltpu.VMEM((rows, width), BF16),
            pltpu.VMEM((rows, HD), BF16),
            pltpu.VMEM((rows, HD), BF16),
            pltpu.VMEM((rows, width), BF16),
            pltpu.VMEM((8, tag_table.shape[0]), F32),
            pltpu.VMEM((n, 8, tag_table.shape[0]), F32),
            pltpu.SemaphoreType.DMA((n,)),
            pltpu.SemaphoreType.DMA((n,)),
            pltpu.SemaphoreType.DMA((9,)),
        ] + attention_scratch(rows, width, plen),
        compiler_params=pltpu.CompilerParams(
            collective_id=0, has_side_effects=True, vmem_limit_bytes=24 * 1024 * 1024),
        name="encode",
    )(*in_hbm(lengths, tag_ids, tag_amounts, tag_table, position_table, prefix_weight, q, k, v, g))


def attend_kernel(me_ref, len_ref, q_ref, k_ref, v_ref, g_ref, prefix_ref, own_out, own_pg, own_bad,
                  q_hbm, k_hbm, v_hbm, g_hbm, out_hbm, pg_ref,
                  outs, bad_scr, oq, ok, ov, og, out_sem, own_sem, *scratch):
    step, last = pl.program_id(0), pl.num_programs(0) - 1
    me = me_ref[0]
    here = lax.rem(me + 1 + step, last + 2)
    slot = lax.rem(step, 2)
    plen = prefix_ref.shape[1]
    vx, pkbd, pvbd = scratch[:3]
    q, k, g, out = q_ref.at[0], k_ref.at[0], g_ref.at[0], outs.at[slot]
    own_copy = pltpu.make_async_copy(own_out, out_hbm.at[me], own_sem.at[0])

    @pl.when(step == 0)
    def _():
        own_copy.start()
        clear(vx, pkbd, pvbd)

    @pl.when(step >= 2)
    def _():
        pltpu.make_async_copy(out, out_hbm.at[here], out_sem.at[slot]).wait()

    length = len_ref[here]
    place(length, prefix_ref[here], v_ref[0], vx, pkbd, pvbd)
    pg_ref[here], bad_scr[...] = attend_fast(length, q, k, g, out, plen, *scratch)

    @pl.when(jnp.max(bad_scr[...]) > 0.0)
    def _():
        pg_ref[here] = attend_exact(length, q, k, g, out, plen, *scratch)

    pltpu.make_async_copy(out, out_hbm.at[here], out_sem.at[slot]).start()

    @pl.when(step == last)
    def _():
        own_copy.wait()
        pg_ref[me] = own_pg[...]
        pltpu.make_async_copy(outs.at[1 - slot], out_hbm.at[here], out_sem.at[1 - slot]).wait()

        @pl.when(jnp.max(own_bad[...]) > 0.0)
        def _():
            loads = [pltpu.make_async_copy(src.at[me], dst, own_sem.at[i]) for i, (src, dst) in enumerate(
                ((q_hbm, oq), (k_hbm, ok), (v_hbm, ov), (g_hbm, og)))]
            for load in loads:
                load.start()
            for load in loads:
                load.wait()
            place(len_ref[me], prefix_ref[me], ov[...], vx, pkbd, pvbd)
            again = outs.at[1 - slot]
            pg_ref[me] = attend_exact(len_ref[me], oq, ok, og, again, plen, *scratch)
            store = pltpu.make_async_copy(again, out_hbm.at[me], own_sem.at[0])
            store.start()
            store.wait()

        pltpu.make_async_copy(out, out_hbm.at[here], out_sem.at[slot]).wait()


def attention(me, lengths, q, k, v, g, prefix, own_out, own_pg, own_bad):
    n, rows, width = q.shape
    plen, cols = prefix.shape[1:]
    spec = lambda shape: pl.BlockSpec((1,) + shape, lambda e, me: (lax.rem(me[0] + 1 + e, n), 0, 0))
    vmem = pl.BlockSpec(memory_space=pltpu.VMEM)
    hbm = pl.BlockSpec(memory_space=pltpu.HBM)
    tokens = in_hbm(q, k, v, g)
    return pl.pallas_call(
        attend_kernel,
        grid_spec=pltpu.PrefetchScalarGridSpec(
            num_scalar_prefetch=1,
            grid=(n - 1,),
            in_specs=[pl.BlockSpec(memory_space=pltpu.SMEM), spec((rows, width)), spec((rows, HD)),
                      spec((rows, HD)), spec((rows, width))] + [vmem] * 4 + [hbm] * 4,
            out_specs=(hbm, vmem),
            scratch_shapes=[
                pltpu.VMEM((2, rows, width), BF16),
                pltpu.VMEM((8, HD), F32),
                pltpu.VMEM((rows, width), BF16),
                pltpu.VMEM((rows, HD), BF16),
                pltpu.VMEM((rows, HD), BF16),
                pltpu.VMEM((rows, width), BF16),
                pltpu.SemaphoreType.DMA((2,)),
                pltpu.SemaphoreType.DMA((4,)),
            ] + attention_scratch(rows, width, plen),
        ),
        out_shape=(pltpu.HBM(q.shape, BF16), pltpu.VMEM((n, plen, cols), F32)),
        compiler_params=pltpu.CompilerParams(vmem_limit_bytes=40 * 1024 * 1024),
        name="attend",
    )(me, *in_hbm(lengths), *tokens, prefix, own_out, own_pg, own_bad, *tokens)


def exchange_kernel(hid, pg, own_ref, all_ref, out_buf, part, landed,
                    sems_pg, sems_rs, sems_ag, sems_core):
    d, t = lax.axis_index("dp"), lax.axis_index("tensor")
    y, zh, core = d // 4, lax.rem(d // 2, 2), lax.rem(d, 2)
    zl, x = t // 4, lax.rem(t, 4)
    z = zh * 2 + zl
    me = dict(x=x, y=y, z=z)

    def device(x, y, z, core):
        return ((y * 2 + z // 2) * 2 + core, lax.rem(z, 2) * 4 + x)

    def shifted(offsets, flip=0):
        c = {axis: lax.rem(me[axis] + offsets.get(axis, 0), 4) for axis in me}
        return device(c["x"], c["y"], c["z"], lax.rem(core + flip, 2))

    def offsets_over(axes):
        out = [{}]
        for axis in axes:
            out = [{**o, axis: i} for o in out for i in range(4)]
        far = lambda o: -sum((0, 1, 2, 1)[i] for i in o.values())
        return sorted([o for o in out if any(o.values())], key=far)

    plane, line = offsets_over("xy"), offsets_over("z")
    others = [{"y": i, "z": j} for i in (2, 1, 3, 0) for j in (2, 0) if i or j]
    sums = [(o, flip) for o in others for flip in (0, 1)] + [({}, 1)]
    tensor = [(d, lax.rem(t + i, 8)) for i in range(1, 8)]
    peers = [shifted(o) for o in plane + line]
    peers += [shifted(o, flip) for o, flip in sums if flip or (o["y"] and o["z"])]
    peers += [(d, lax.rem(zl + 1, 2) * 4 + lax.rem(x + i, 4)) for i in (1, 2, 3)]
    barrier = pltpu.get_barrier_semaphore()
    for peer in peers:
        pl.semaphore_signal(barrier, inc=1, device_id=peer, device_id_type=MESH)
    grads = pg[...]
    high = grads.astype(BF16)
    out_buf[...] = high
    own_ref[t] = out_buf[t]
    flat_high = high.reshape(-1, high.shape[2])
    low = (grads.reshape(flat_high.shape) - flat_high.astype(F32)).astype(BF16)
    total = dot(hid[...], flat_high, TN) + dot(hid[...], low, TN)
    part[...] = total.astype(BF16).reshape(part.shape)
    pl.semaphore_wait(barrier, len(peers))

    def send(src, dst, sems, i, peer):
        copy = pltpu.make_async_remote_copy(
            src_ref=src, dst_ref=dst, send_sem=sems.at[0, i], recv_sem=sems.at[1, i],
            device_id=peer, device_id_type=MESH)
        copy.start()
        return copy

    scatter = []
    for i, (o, flip) in enumerate(sums):
        to = shifted(o, flip)
        scatter.append(send(part.at[to[0]], landed.at[i], sems_rs, i, to))
    back = [send(out_buf.at[to[1]], own_ref.at[t], sems_pg, i, to) for i, to in enumerate(tensor)]
    chunk = part[d].astype(F32)
    for i, copy in enumerate(scatter):
        copy.wait()
        chunk += landed[i].astype(F32)
    chunk = (chunk * (1.0 / SEQS)).astype(BF16)
    half = chunk.shape[1] // 2
    all_ref[0, core, z, y, x] = chunk[:, :half]
    all_ref[1, core, y, x, z] = chunk[:, half:]
    first = [send(all_ref.at[0, core, z, y, x], all_ref.at[0, core, z, y, x], sems_ag, i, shifted(o))
             for i, o in enumerate(plane)]
    first += [send(all_ref.at[1, core, y, x, z], all_ref.at[1, core, y, x, z], sems_ag, 15 + i, shifted(o))
              for i, o in enumerate(line)]
    for copy in first[15:]:
        copy.wait()
    wide = [send(all_ref.at[1, core, y, x], all_ref.at[1, core, y, x], sems_ag, 18 + i, shifted(o))
            for i, o in enumerate(plane)]
    for copy in first[:15]:
        copy.wait()
    deep = [send(all_ref.at[0, core, z], all_ref.at[0, core, z], sems_ag, 33 + i, shifted(o))
            for i, o in enumerate(line)]
    sibling = shifted({}, 1)
    passed = [send(all_ref.at[0, core, z], all_ref.at[0, core, z], sems_core, 0, sibling)]
    for o, copy in zip(line, deep):
        copy.wait()
        block = all_ref.at[0, core, lax.rem(z + 4 - o["z"], 4)]
        passed.append(send(block, block, sems_core, o["z"], sibling))
    for i in (2, 1, 3, 0):
        for o, copy in zip(plane, wide):
            if o["y"] == i:
                copy.wait()
        block = all_ref.at[1, core, lax.rem(y + 4 - i, 4)]
        passed.append(send(block, block, sems_core, 4 + i, sibling))
    for copy in passed + back:
        copy.wait()


def exchange(hidden, pgrads):
    n, plen, cols = pgrads.shape
    width = hidden.shape[1]
    rows = width // 16
    vmem = pl.BlockSpec(memory_space=pltpu.VMEM)
    return pl.pallas_call(
        exchange_kernel,
        out_shape=(pltpu.VMEM((n, plen, cols), BF16), pltpu.VMEM((2, 2, 4, 4, 4, rows, cols // 2), BF16)),
        in_specs=[vmem] * 2,
        out_specs=(vmem, vmem),
        scratch_shapes=[
            pltpu.VMEM((n, plen, cols), BF16),
            pltpu.VMEM((16, rows, cols), BF16),
            pltpu.VMEM((16, rows, cols), BF16),
            pltpu.SemaphoreType.DMA((2, 8)),
            pltpu.SemaphoreType.DMA((2, 16)),
            pltpu.SemaphoreType.DMA((2, 36)),
            pltpu.SemaphoreType.DMA((2, 8)),
        ],
        compiler_params=pltpu.CompilerParams(collective_id=1, has_side_effects=True, vmem_limit_bytes=16 * 1024 * 1024),
        name="exchange",
    )(hidden, pgrads)


def finish_kernel(own_ref, first_ref, second_ref, prefix_grad_ref, weight_grad_ref):
    cols = own_ref.shape[2]
    half = cols // 2
    for j in range(own_ref.shape[0]):
        prefix_grad_ref[0, :, j * cols:(j + 1) * cols] = own_ref[j].astype(F32)
    ys, rows = first_ref.shape[3], first_ref.shape[5]
    for y in range(ys):
        for core in range(2):
            for z in range(4):
                r0 = ((y * 2 + z // 2) * 2 + core) * rows
                for x in range(4):
                    c0 = ((z % 2) * 4 + x) * cols
                    weight_grad_ref[r0:r0 + rows, c0:c0 + half] = first_ref[0, core, z, y, x].astype(F32)
                    weight_grad_ref[r0:r0 + rows, c0 + half:c0 + cols] = second_ref[0, core, y, x, z].astype(F32)


def finish(own, gathered, steps=2):
    n, plen, cols = own.shape
    rows = gathered.shape[5]
    ys = 4 // steps
    return pl.pallas_call(
        finish_kernel,
        grid=(steps,),
        out_shape=(pltpu.HBM((1, plen, n * cols), F32), pltpu.HBM((16 * rows, n * cols), F32)),
        in_specs=[pl.BlockSpec((n // steps, plen, cols), lambda i: (i, 0, 0)),
                  pl.BlockSpec((1, 2, 4, ys, 4, rows, cols // 2), lambda i: (0, 0, 0, i, 0, 0, 0)),
                  pl.BlockSpec((1, 2, ys, 4, 4, rows, cols // 2), lambda i: (1, 0, i, 0, 0, 0, 0))],
        out_specs=(pl.BlockSpec((1, plen, n // steps * cols), lambda i: (0, 0, i)),
                   pl.BlockSpec((4 * ys * rows, n * cols), lambda i: (i, 0))),
        compiler_params=pltpu.CompilerParams(vmem_limit_bytes=24 * 1024 * 1024),
        name="widen",
    )(own, gathered, gathered)


def shards(tag_ids, tag_amounts, tag_table, position_table, prefix_weight,
           query_own, key_own, value_own, out_grad, seq_lengths):
    tokens = (query_own, key_own, value_own, out_grad)
    prefix, hidden, own_out, own_pg, own_bad, me = encode(
        seq_lengths, tag_ids, tag_amounts, tag_table, position_table, prefix_weight, *tokens)
    attn_out, pgrads = attention(me, seq_lengths, *tokens, prefix, own_out, own_pg, own_bad)
    prefix_grad, weight_grad = finish(*exchange(hidden, pgrads))
    return attn_out, prefix_grad, weight_grad


def solution(mesh):
    return jax.shard_map(
        shards,
        mesh=mesh,
        in_specs=(
            P(("dp", "tensor"), None),
            P(("dp", "tensor"), None),
            P(),
            P(),
            P(),
            P("dp", None, "tensor"),
            P("dp", None, "tensor"),
            P("dp", None, "tensor"),
            P("dp", None, "tensor"),
            P("dp"),
        ),
        out_specs=(P("dp", None, "tensor"), P(("dp", "tensor"), None, None), P()),
        check_vma=False,
    )
```

time: 205 us -> 203 us (level)
    pallas_call x4, Pallas kernels: 204 us -> 202 us  [the longest x1 166 us: attention(): pl.pallas_call(attend_kernel, grid_spec=pltpu.PrefetchScalarGridSpec(num_...]
where the time goes in v3:
time: 203 us
  Pallas kernels  202 us (100%)
    pallas_call x1, Pallas kernels, attention(): pl.pallas_call(attend_kernel, grid_spec=pltpu.PrefetchScalarGridSpec(num_...  166 us
    pallas_call x1, Pallas kernels, exchange(): pl.pallas_call(exchange_kernel, out_shape=(pltpu.VMEM((n, plen, cols), BF...  24.7 us
    pallas_call x1, Pallas kernels, encode(): pl.pallas_call(functools.partial(encode_kernel, n), out_shape=(pltpu.VMEM...  9.66 us

profile of v3, /device:TPU:1, one launch (start us, length us, event | category | flops | bytes accessed | tf_op | source)
XLA Modules:
  0.0 202.6 jit_solution(8296678986684590501)
XLA Ops:
  0.6 9.7 %encode.1 = (bf16[8,32,256]{2,1,0:T(8,128)(2,1)S(1)}, bf16[256,256]{1,0:T(8,128)(2,1)S(1)}, bf16[768,512]{1,0:T(8,128)(2,1)S(1)}, f32[32,256]{1,0:T(8,128)S(1)}, f32[8,128]{1,0:T(8,128)S(1)}, /*index=5*/s32[1]{0:T(128)}) custom-call(s32[8]{0:T(128)} %len_ref.3, s32[1,8]{1,0:T(1,128)} %ids_hbm.1, f32[1,8]{1,0:T(1,128)} %amt_hbm.1, ...), custom_call_target="tpu_custom_call" | custom-call | tf_op jit(solution)/shard_map/encode/pallas_call | solution.py:261
  10.3 166.0 %attend.1 = (bf16[8,768,512]{2,1,0:T(8,128)(2,1)}, f32[8,32,256]{2,1,0:T(8,128)S(1)}) custom-call(s32[1]{0:T(128)} %get-tuple-element.15.me_ref, s32[8]{0:T(128)} %len_ref.3, bf16[8,768,512]{2,1,0:T(8,128)(2,1)} %q_hbm.3, bf16[8,768,128]{2,1,0:T(8,128)(2,1)} %k_hbm.3, bf16[8,768,128]{2,1,0:T(8,128)(2,1)} %v_hbm.3, bf16[8,768,512]{2,1,0:T(8,128)(2,1)} %g_hbm.3, ...), custom_call_target="tpu_custom_call" | custom-call | tf_op jit(solution)/shard_map/attend/pallas_call | solution.py:352
  176.3 24.7 %exchange.1 = (bf16[8,32,256]{2,1,0:T(8,128)(2,1)S(1)}, bf16[2,2,4,4,4,16,128]{6,5,4,3,2,1,0:T(8,128)(2,1)S(1)}) custom-call(bf16[256,256]{1,0:T(8,128)(2,1)S(1)} %get-tuple-element.21.hid, f32[8,32,256]{2,1,0:T(8,128)S(1)} %get-tuple-element.22.pg), custom_call_target="tpu_custom_call" | custom-call | tf_op jit(solution)/shard_map/exchange/pallas_call | solution.py:472
  201.0 1.6 widen.1

commit v4 on v3

--- a/solution.py
+++ b/solution.py
@@ -31,14 +31,14 @@
     return jnp.concatenate([jnp.tanh(pos + pooled[j:j + 1]) for j in range(mixture.shape[0])], 0).astype(BF16)
 
 
-def attention_scratch(rows, width, plen):
+def attention_scratch(rows, width, plen, sets=()):
     seg_w = width // HD * plen
     return [
         pltpu.VMEM((seg_w + rows, 2 * HD), BF16),
         pltpu.VMEM((seg_w, width), BF16),
         pltpu.VMEM((seg_w, width), BF16),
-        pltpu.VMEM((rows, seg_w), BF16),
-        pltpu.VMEM((rows, seg_w), BF16),
+        pltpu.VMEM((*sets, rows, seg_w), BF16),
+        pltpu.VMEM((*sets, rows, seg_w), BF16),
         pltpu.VMEM((rows, seg_w), F32),
     ]
 
@@ -90,7 +90,7 @@
 
 
 def attend_fast(length, q_ref, k_ref, g_ref, out_ref, plen, vx, pkbd, pvbd, ds_scr, w_scr, pp_scr,
-                nr=128, groups=2, late=2):
+                beside=None, nr=128, groups=2, late=2):
     rows, width = q_ref.shape
     heads = width // HD
     seg_w = heads * plen
@@ -142,6 +142,8 @@
     bad = jnp.zeros((8, HD), F32)
     starts = list(range(0, rows, nr))
     state = score_phase(starts[0])
+    if beside is not None:
+        beside()
     for i, r0 in enumerate(starts):
         now = state
         if i + 1 < len(starts):
@@ -152,7 +154,7 @@
         g = g_ref[r0:r0 + step]
         delta = row_delta(g, out_ref[r0:r0 + step], plen)
         ds_scr[r0:r0 + step] = (pp_scr[r0:r0 + step] * (dot(g, pvbd[...], NT) - delta)).astype(BF16)
-    return prefix_gradient(q_ref, g_ref, ds_scr, w_scr, plen), bad
+    return bad
 
 
 def attend_exact(length, q_ref, k_ref, g_ref, out_ref, plen, vx, pkbd, pvbd, ds_scr, w_scr, pp_scr):
@@ -194,11 +196,10 @@
         return carry
 
     lax.fori_loop(0, rows // nr, block, 0)
-    return prefix_gradient(q_ref, g_ref, ds_scr, w_scr, plen)
 
 
 def encode_kernel(n, len_ref, ids_hbm, amt_hbm, table_hbm, pos_hbm, weight_hbm, q_hbm, k_hbm, v_hbm, g_hbm,
-                  prefix_ref, hidden_ref, out_ref, pg_ref, bad_ref, me_ref,
+                  prefix_ref, hidden_ref, out_ref, pg_ref, bad_ref, nq, nk, nv, ng, me_ref,
                   ids_ref, amt_ref, table_ref, pos_ref, wbuf, q_ref, k_ref, v_ref, g_ref, mine, got,
                   send_sem, recv_sem, load_sem, *scratch):
     d, t = lax.axis_index("dp"), lax.axis_index("tensor")
@@ -208,11 +209,17 @@
         (ids_hbm, ids_ref), (amt_hbm, amt_ref), (table_hbm, table_ref), (pos_hbm, pos_ref),
         (weight_hbm.at[:, pl.ds(pl.multiple_of(t * cols, cols), cols)], wbuf),
         (q_hbm.at[t], q_ref), (k_hbm.at[t], k_ref), (v_hbm.at[t], v_ref), (g_hbm.at[t], g_ref)))]
+    after = lax.rem(t + 1, n)
+    ahead = [pltpu.make_async_copy(src.at[after], dst, load_sem.at[9 + i]) for i, (src, dst) in enumerate((
+        (q_hbm, nq.at[0]), (k_hbm, nk.at[0]), (v_hbm, nv.at[0]), (g_hbm, ng.at[0])))]
     for load in loads:
         load.start()
     barrier = pltpu.get_barrier_semaphore()
-    for i in range(1, n):
-        pl.semaphore_signal(barrier, inc=1, device_id=(d, lax.rem(t + i, n)), device_id_type=MESH)
+    line = n // 2
+    peers = [(d, lax.rem(t // line + a, 2) * line + lax.rem(t + b, line))
+             for a, b in ((1, 2), (1, 1), (1, 3), (0, 2), (1, 0), (0, 1), (0, 3))]
+    for peer in peers:
+        pl.semaphore_signal(barrier, inc=1, device_id=peer, device_id_type=MESH)
     loads[0].wait()
     loads[1].wait()
     tags = table_ref.shape[0]
@@ -233,22 +240,27 @@
     own = dot(hidden_of(mix, table_ref[...], pos_ref[...]), wbuf[...]).astype(BF16)
     pl.semaphore_wait(barrier, n - 1)
     copies = []
-    for i in range(1, n):
+    for i, peer in enumerate(peers):
         copy = pltpu.make_async_remote_copy(
             src_ref=mine, dst_ref=got.at[t], send_sem=send_sem.at[i], recv_sem=recv_sem.at[i],
-            device_id=(d, lax.rem(t + i, n)), device_id_type=MESH)
+            device_id=peer, device_id_type=MESH)
         copy.start()
         copies.append(copy)
     for load in loads[5:]:
         load.wait()
+    for load in ahead:
+        load.start()
     place(length, own, v_ref[...], vx, pkbd, pvbd)
-    pg_ref[...], bad_ref[...] = attend_fast(length, q_ref, k_ref, g_ref, out_ref, plen, *scratch)
+    bad_ref[...] = attend_fast(length, q_ref, k_ref, g_ref, out_ref, plen, *scratch)
+    pg_ref[...] = prefix_gradient(q_ref, g_ref, ds_scr, w_scr, plen)
     for copy in copies:
         copy.wait()
     mixture = jnp.concatenate([got[j, 0:1] for j in range(n)], 0)
     hidden = hidden_of(mixture, table_ref[...], pos_ref[...])
     hidden_ref[...] = hidden
     prefix_ref[...] = dot(hidden, wbuf[...]).astype(BF16).reshape(prefix_ref.shape)
+    for load in ahead:
+        load.wait()
 
 
 def encode(lengths, tag_ids, tag_amounts, tag_table, position_table, prefix_weight, q, k, v, g):
@@ -262,9 +274,12 @@
         functools.partial(encode_kernel, n),
         out_shape=(pltpu.VMEM((n, plen, cols), BF16), pltpu.VMEM((n * plen, units), BF16),
                    pltpu.VMEM((rows, width), BF16), pltpu.VMEM((plen, cols), F32),
-                   pltpu.VMEM((8, HD), F32), jax.ShapeDtypeStruct((1,), jnp.int32)),
+                   pltpu.VMEM((8, HD), F32),
+                   pltpu.VMEM((3, rows, width), BF16), pltpu.VMEM((3, rows, HD), BF16),
+                   pltpu.VMEM((3, rows, HD), BF16), pltpu.VMEM((3, rows, width), BF16),
+                   jax.ShapeDtypeStruct((1,), jnp.int32)),
         in_specs=[smem] + [pl.BlockSpec(memory_space=pltpu.HBM)] * 9,
-        out_specs=(vmem,) * 5 + (smem,),
+        out_specs=(vmem,) * 9 + (smem,),
         scratch_shapes=[
             pltpu.VMEM(tag_ids.shape, jnp.int32),
             pltpu.VMEM(tag_amounts.shape, F32),
@@ -279,7 +294,7 @@
             pltpu.VMEM((n, 8, tag_table.shape[0]), F32),
             pltpu.SemaphoreType.DMA((n,)),
             pltpu.SemaphoreType.DMA((n,)),
-            pltpu.SemaphoreType.DMA((9,)),
+            pltpu.SemaphoreType.DMA((13,)),
         ] + attention_scratch(rows, width, plen),
         compiler_params=pltpu.CompilerParams(
             collective_id=0, has_side_effects=True, vmem_limit_bytes=24 * 1024 * 1024),
@@ -287,91 +302,115 @@
     )(*in_hbm(lengths, tag_ids, tag_amounts, tag_table, position_table, prefix_weight, q, k, v, g))
 
 
-def attend_kernel(me_ref, len_ref, q_ref, k_ref, v_ref, g_ref, prefix_ref, own_out, own_pg, own_bad,
-                  q_hbm, k_hbm, v_hbm, g_hbm, out_hbm, pg_ref,
-                  outs, bad_scr, oq, ok, ov, og, out_sem, own_sem, *scratch):
+def attend_kernel(me_ref, len_ref, prefix_ref, own_out, own_pg, own_bad, _q, _k, _v, _g,
+                  q_hbm, k_hbm, v_hbm, g_hbm, out_hbm, pg_ref, qs, ks, vs, gs,
+                  outs, bad_scr, rq, rk, rv, rg, out_sem, in_sem, own_sem, redo_sem,
+                  vx, pkbd, pvbd, ds_scr, w_scr, pp_scr):
     step, last = pl.program_id(0), pl.num_programs(0) - 1
     me = me_ref[0]
     here = lax.rem(me + 1 + step, last + 2)
-    slot = lax.rem(step, 2)
+    before = lax.rem(me + step, last + 2)
+    slot, even = lax.rem(step, 3), lax.rem(step, 2)
+    gone = lax.rem(step + 2, 3)
     plen = prefix_ref.shape[1]
-    vx, pkbd, pvbd = scratch[:3]
-    q, k, g, out = q_ref.at[0], k_ref.at[0], g_ref.at[0], outs.at[slot]
-    own_copy = pltpu.make_async_copy(own_out, out_hbm.at[me], own_sem.at[0])
+    out = outs.at[even]
+    own_copy = pltpu.make_async_copy(own_out, out_hbm.at[me], own_sem)
+
+    def loads(example, into):
+        return [pltpu.make_async_copy(src.at[example], dst.at[into], in_sem.at[into, i])
+                for i, (src, dst) in enumerate(((q_hbm, qs), (k_hbm, ks), (v_hbm, vs), (g_hbm, gs)))]
+
+    def store(into):
+        return pltpu.make_async_copy(outs.at[into], out_hbm.at[here], out_sem.at[into])
 
     @pl.when(step == 0)
     def _():
         own_copy.start()
         clear(vx, pkbd, pvbd)
 
+    @pl.when(step > 0)
+    def _():
+        for load in loads(here, slot):
+            load.wait()
+
+    @pl.when(step < last)
+    def _():
+        for load in loads(lax.rem(here + 1, last + 2), lax.rem(step + 1, 3)):
+            load.start()
+
     @pl.when(step >= 2)
     def _():
-        pltpu.make_async_copy(out, out_hbm.at[here], out_sem.at[slot]).wait()
+        store(even).wait()
+
+    def previous():
+        pg_ref[before] = prefix_gradient(qs.at[gone], gs.at[gone], ds_scr.at[1 - even], w_scr.at[1 - even], plen)
 
     length = len_ref[here]
-    place(length, prefix_ref[here], v_ref[0], vx, pkbd, pvbd)
-    pg_ref[here], bad_scr[...] = attend_fast(length, q, k, g, out, plen, *scratch)
+    place(length, prefix_ref[here], vs[slot], vx, pkbd, pvbd)
+    scratch = (vx, pkbd, pvbd, ds_scr.at[even], w_scr.at[even], pp_scr)
+    bad_scr[...] = attend_fast(length, qs.at[slot], ks.at[slot], gs.at[slot], out, plen, *scratch, beside=previous)
 
     @pl.when(jnp.max(bad_scr[...]) > 0.0)
     def _():
-        pg_ref[here] = attend_exact(length, q, k, g, out, plen, *scratch)
-
-    pltpu.make_async_copy(out, out_hbm.at[here], out_sem.at[slot]).start()
+        attend_exact(length, qs.at[slot], ks.at[slot], gs.at[slot], out, plen, *scratch)
+
+    store(even).start()
 
     @pl.when(step == last)
     def _():
         own_copy.wait()
+        pg_ref[here] = prefix_gradient(qs.at[slot], gs.at[slot], ds_scr.at[even], w_scr.at[even], plen)
         pg_ref[me] = own_pg[...]
-        pltpu.make_async_copy(outs.at[1 - slot], out_hbm.at[here], out_sem.at[1 - slot]).wait()
+        store(1 - even).wait()
 
         @pl.when(jnp.max(own_bad[...]) > 0.0)
         def _():
-            loads = [pltpu.make_async_copy(src.at[me], dst, own_sem.at[i]) for i, (src, dst) in enumerate(
-                ((q_hbm, oq), (k_hbm, ok), (v_hbm, ov), (g_hbm, og)))]
-            for load in loads:
-                load.start()
-            for load in loads:
-                load.wait()
-            place(len_ref[me], prefix_ref[me], ov[...], vx, pkbd, pvbd)
-            again = outs.at[1 - slot]
-            pg_ref[me] = attend_exact(len_ref[me], oq, ok, og, again, plen, *scratch)
-            store = pltpu.make_async_copy(again, out_hbm.at[me], own_sem.at[0])
-            store.start()
-            store.wait()
-
-        pltpu.make_async_copy(out, out_hbm.at[here], out_sem.at[slot]).wait()
-
-
-def attention(me, lengths, q, k, v, g, prefix, own_out, own_pg, own_bad):
+            copies = [pltpu.make_async_copy(src.at[me], dst, redo_sem.at[i]) for i, (src, dst) in enumerate(
+                ((q_hbm, rq), (k_hbm, rk), (v_hbm, rv), (g_hbm, rg)))]
+            for copy in copies:
+                copy.start()
+            for copy in copies:
+                copy.wait()
+            place(len_ref[me], prefix_ref[me], rv[...], vx, pkbd, pvbd)
+            attend_exact(len_ref[me], rq, rk, rg, outs.at[1 - even], plen, *scratch)
+            pg_ref[me] = prefix_gradient(rq, rg, ds_scr.at[even], w_scr.at[even], plen)
+            again = pltpu.make_async_copy(outs.at[1 - even], out_hbm.at[me], own_sem)
+            again.start()
+            again.wait()
+
+        store(even).wait()
+
+
+def attention(me, lengths, q, k, v, g, prefix, own_out, own_pg, own_bad, ahead):
     n, rows, width = q.shape
     plen, cols = prefix.shape[1:]
-    spec = lambda shape: pl.BlockSpec((1,) + shape, lambda e, me: (lax.rem(me[0] + 1 + e, n), 0, 0))
+    smem = pl.BlockSpec(memory_space=pltpu.SMEM)
     vmem = pl.BlockSpec(memory_space=pltpu.VMEM)
     hbm = pl.BlockSpec(memory_space=pltpu.HBM)
-    tokens = in_hbm(q, k, v, g)
+    wide, narrow = (rows, width), (rows, HD)
     return pl.pallas_call(
         attend_kernel,
-        grid_spec=pltpu.PrefetchScalarGridSpec(
-            num_scalar_prefetch=1,
-            grid=(n - 1,),
-            in_specs=[pl.BlockSpec(memory_space=pltpu.SMEM), spec((rows, width)), spec((rows, HD)),
-                      spec((rows, HD)), spec((rows, width))] + [vmem] * 4 + [hbm] * 4,
-            out_specs=(hbm, vmem),
-            scratch_shapes=[
-                pltpu.VMEM((2, rows, width), BF16),
-                pltpu.VMEM((8, HD), F32),
-                pltpu.VMEM((rows, width), BF16),
-                pltpu.VMEM((rows, HD), BF16),
-                pltpu.VMEM((rows, HD), BF16),
-                pltpu.VMEM((rows, width), BF16),
-                pltpu.SemaphoreType.DMA((2,)),
-                pltpu.SemaphoreType.DMA((4,)),
-            ] + attention_scratch(rows, width, plen),
-        ),
-        out_shape=(pltpu.HBM(q.shape, BF16), pltpu.VMEM((n, plen, cols), F32)),
+        grid=(n - 1,),
+        in_specs=[smem, smem] + [vmem] * 8 + [hbm] * 4,
+        out_specs=(hbm,) + (vmem,) * 5,
+        scratch_shapes=[
+            pltpu.VMEM((2, *wide), BF16),
+            pltpu.VMEM((8, HD), F32),
+            pltpu.VMEM(wide, BF16),
+            pltpu.VMEM(narrow, BF16),
+            pltpu.VMEM(narrow, BF16),
+            pltpu.VMEM(wide, BF16),
+            pltpu.SemaphoreType.DMA((2,)),
+            pltpu.SemaphoreType.DMA((3, 4)),
+            pltpu.SemaphoreType.DMA,
+            pltpu.SemaphoreType.DMA((4,)),
+        ] + attention_scratch(rows, width, plen, (2,)),
+        out_shape=(pltpu.HBM(q.shape, BF16), pltpu.VMEM((n, plen, cols), F32),
+                   *(pltpu.VMEM(buf.shape, BF16) for buf in ahead)),
+        input_output_aliases={6 + i: 2 + i for i in range(4)},
         compiler_params=pltpu.CompilerParams(vmem_limit_bytes=40 * 1024 * 1024),
         name="attend",
-    )(me, *in_hbm(lengths), *tokens, prefix, own_out, own_pg, own_bad, *tokens)
+    )(me, *in_hbm(lengths), prefix, own_out, own_pg, own_bad, *ahead, *in_hbm(q, k, v, g))
 
 
 def exchange_kernel(hid, pg, own_ref, all_ref, out_buf, part, landed,
@@ -389,20 +428,22 @@
         c = {axis: lax.rem(me[axis] + offsets.get(axis, 0), 4) for axis in me}
         return device(c["x"], c["y"], c["z"], lax.rem(core + flip, 2))
 
+    far = lambda o: -sum((0, 1, 2, 1)[i] for i in o.values())
+
     def offsets_over(axes):
         out = [{}]
         for axis in axes:
             out = [{**o, axis: i} for o in out for i in range(4)]
-        far = lambda o: -sum((0, 1, 2, 1)[i] for i in o.values())
         return sorted([o for o in out if any(o.values())], key=far)
 
     plane, line = offsets_over("xy"), offsets_over("z")
     others = [{"y": i, "z": j} for i in (2, 1, 3, 0) for j in (2, 0) if i or j]
     sums = [(o, flip) for o in others for flip in (0, 1)] + [({}, 1)]
     tensor = [(d, lax.rem(t + i, 8)) for i in range(1, 8)]
-    peers = [shifted(o) for o in plane + line]
-    peers += [shifted(o, flip) for o, flip in sums if flip or (o["y"] and o["z"])]
-    peers += [(d, lax.rem(zl + 1, 2) * 4 + lax.rem(x + i, 4)) for i in (1, 2, 3)]
+    peers = [(far(o), shifted(o)) for o in plane + line]
+    peers += [(far(o), shifted(o, flip)) for o, flip in sums if flip or (o["y"] and o["z"])]
+    peers += [(-1 - (0, 1, 2, 1)[i], (d, lax.rem(zl + 1, 2) * 4 + lax.rem(x + i, 4))) for i in (1, 2, 3)]
+    peers = [peer for _, peer in sorted(peers, key=lambda item: item[0])]
     barrier = pltpu.get_barrier_semaphore()
     for peer in peers:
         pl.semaphore_signal(barrier, inc=1, device_id=peer, device_id_type=MESH)
@@ -436,15 +477,15 @@
     half = chunk.shape[1] // 2
     all_ref[0, core, z, y, x] = chunk[:, :half]
     all_ref[1, core, y, x, z] = chunk[:, half:]
-    first = [send(all_ref.at[0, core, z, y, x], all_ref.at[0, core, z, y, x], sems_ag, i, shifted(o))
+    early = [send(all_ref.at[1, core, y, x, z], all_ref.at[1, core, y, x, z], sems_ag, i, shifted(o))
+             for i, o in enumerate(line)]
+    first = [send(all_ref.at[0, core, z, y, x], all_ref.at[0, core, z, y, x], sems_ag, 3 + i, shifted(o))
              for i, o in enumerate(plane)]
-    first += [send(all_ref.at[1, core, y, x, z], all_ref.at[1, core, y, x, z], sems_ag, 15 + i, shifted(o))
-              for i, o in enumerate(line)]
-    for copy in first[15:]:
+    for copy in early:
         copy.wait()
     wide = [send(all_ref.at[1, core, y, x], all_ref.at[1, core, y, x], sems_ag, 18 + i, shifted(o))
             for i, o in enumerate(plane)]
-    for copy in first[:15]:
+    for copy in first:
         copy.wait()
     deep = [send(all_ref.at[0, core, z], all_ref.at[0, core, z], sems_ag, 33 + i, shifted(o))
             for i, o in enumerate(line)]
@@ -525,9 +566,9 @@
 def shards(tag_ids, tag_amounts, tag_table, position_table, prefix_weight,
            query_own, key_own, value_own, out_grad, seq_lengths):
     tokens = (query_own, key_own, value_own, out_grad)
-    prefix, hidden, own_out, own_pg, own_bad, me = encode(
+    prefix, hidden, own_out, own_pg, own_bad, *ahead, me = encode(
         seq_lengths, tag_ids, tag_amounts, tag_table, position_table, prefix_weight, *tokens)
-    attn_out, pgrads = attention(me, seq_lengths, *tokens, prefix, own_out, own_pg, own_bad)
+    attn_out, pgrads, *_ = attention(me, seq_lengths, *tokens, prefix, own_out, own_pg, own_bad, ahead)
     prefix_grad, weight_grad = finish(*exchange(hidden, pgrads))
     return attn_out, prefix_grad, weight_grad
 

time: 203 us -> 199 us (0.980)
  Pallas kernels: 202 us -> 198 us
    pallas_call x1, Pallas kernels: 166 us -> 162 us  [attention(): pl.pallas_call(attend_kernel, grid=(n - 1,), in_specs=[smem, smem] + [vme...]
where the time goes in v4:
time: 199 us
  Pallas kernels  198 us (99%)
    pallas_call x1, Pallas kernels, attention(): pl.pallas_call(attend_kernel, grid=(n - 1,), in_specs=[smem, smem] + [vme...  162 us
    pallas_call x1, Pallas kernels, exchange(): pl.pallas_call(exchange_kernel, out_shape=(pltpu.VMEM((n, plen, cols), BF...  24 us
    pallas_call x1, Pallas kernels, encode(): pl.pallas_call(functools.partial(encode_kernel, n), out_shape=(pltpu.VMEM...  10.4 us

profile of v4, /device:TPU:1, one launch (start us, length us, event | category | flops | bytes accessed | tf_op | source)
XLA Modules:
  0.0 198.9 jit_solution(12159653311645701988)
XLA Ops:
  0.6 10.4 %encode.1 = (bf16[8,32,256]{2,1,0:T(8,128)(2,1)S(1)}, bf16[256,256]{1,0:T(8,128)(2,1)S(1)}, bf16[768,512]{1,0:T(8,128)(2,1)S(1)}, f32[32,256]{1,0:T(8,128)S(1)},...) custom-call(s32[8]{0:T(128)} %len_ref.3, ...), custom_call_target="tpu_custom_call" | custom-call | tf_op jit(solution)/shard_map/encode/pallas_call | solution.py:273
  11.0 162.3 %attend.1 = (bf16[8,768,512]{2,1,0:T(8,128)(2,1)}, f32[8,32,256]{2,1,0:T(8,128)S(1)}, bf16[3,768,512]{2,1,0:T(8,128)(2,1)S(1)}, bf16[3,768,128]{2,1,0:T(8,128)(2...) custom-call(s32[1]{0:T(128)} %get-tuple-element.19.me_ref, ...), custom_call_target="tpu_custom_call", output_to_operand_aliasing={{2}: (6, {}), {3}: (7, {}), {4}: (8, {}), {5}: (9, {})} | custom-call | tf_op jit(solution)/shard_map/attend/pallas_call | solution.py:391
  173.3 24.0 %exchange.1 = (bf16[8,32,256]{2,1,0:T(8,128)(2,1)S(1)}, bf16[2,2,4,4,4,16,128]{6,5,4,3,2,1,0:T(8,128)(2,1)S(1)}) custom-call(bf16[256,256]{1,0:T(8,128)(2,1)S(1)} %get-tuple-element.29.hid, f32[8,32,256]{2,1,0:T(8,128)S(1)} %get-tuple-element.30.pg), custom_call_target="tpu_custom_call" | custom-call | tf_op jit(solution)/shard_map/exchange/pallas_call | solution.py:513
  197.3 1.6 widen.1

commit v5 on v4

--- a/solution.py
+++ b/solution.py
@@ -142,12 +142,12 @@
     bad = jnp.zeros((8, HD), F32)
     starts = list(range(0, rows, nr))
     state = score_phase(starts[0])
-    if beside is not None:
-        beside()
     for i, r0 in enumerate(starts):
         now = state
         if i + 1 < len(starts):
             state = score_phase(starts[i + 1])
+        if i == 0 and beside is not None:
+            beside()
         bad = value_phase(r0, *now, bad)
     step = rows // late
     for r0 in range(0, rows, step):

time: 199 us -> 199 us (level)
  no operation moved by 1% of the time
where the time goes in v5:
time: 199 us
  Pallas kernels  198 us (99%)
    pallas_call x1, Pallas kernels, attention(): pl.pallas_call(attend_kernel, grid=(n - 1,), in_specs=[smem, smem] + [vme...  162 us
    pallas_call x1, Pallas kernels, exchange(): pl.pallas_call(exchange_kernel, out_shape=(pltpu.VMEM((n, plen, cols), BF...  24 us
    pallas_call x1, Pallas kernels, encode(): pl.pallas_call(functools.partial(encode_kernel, n), out_shape=(pltpu.VMEM...  10.4 us

profile of v5, /device:TPU:1, one launch (start us, length us, event | category | flops | bytes accessed | tf_op | source)
XLA Modules:
  0.0 198.8 jit_solution(9322291187758654819)
XLA Ops:
  0.6 10.4 %encode.1 = (bf16[8,32,256]{2,1,0:T(8,128)(2,1)S(1)}, bf16[256,256]{1,0:T(8,128)(2,1)S(1)}, bf16[768,512]{1,0:T(8,128)(2,1)S(1)}, f32[32,256]{1,0:T(8,128)S(1)},...) custom-call(s32[8]{0:T(128)} %len_ref.3, ...), custom_call_target="tpu_custom_call" | custom-call | tf_op jit(solution)/shard_map/encode/pallas_call | solution.py:273
  11.0 162.2 %attend.1 = (bf16[8,768,512]{2,1,0:T(8,128)(2,1)}, f32[8,32,256]{2,1,0:T(8,128)S(1)}, bf16[3,768,512]{2,1,0:T(8,128)(2,1)S(1)}, bf16[3,768,128]{2,1,0:T(8,128)(2...) custom-call(s32[1]{0:T(128)} %get-tuple-element.19.me_ref, ...), custom_call_target="tpu_custom_call", output_to_operand_aliasing={{2}: (6, {}), {3}: (7, {}), {4}: (8, {}), {5}: (9, {})} | custom-call | tf_op jit(solution)/shard_map/attend/pallas_call | solution.py:391
  173.2 24.0 %exchange.1 = (bf16[8,32,256]{2,1,0:T(8,128)(2,1)S(1)}, bf16[2,2,4,4,4,16,128]{6,5,4,3,2,1,0:T(8,128)(2,1)S(1)}) custom-call(bf16[256,256]{1,0:T(8,128)(2,1)S(1)} %get-tuple-element.29.hid, f32[8,32,256]{2,1,0:T(8,128)S(1)} %get-tuple-element.30.pg), custom_call_target="tpu_custom_call" | custom-call | tf_op jit(solution)/shard_map/exchange/pallas_call | solution.py:513
  197.2 1.6 widen.1
